TPU v7x, 32 devices: a whole 2x2x4 slice. The times are simulated.
32 devices in a mesh: stream: 2 (over core), clip: 4 (over z), tm: 4 (over y, x).
Axes of the slice: x: 2, y: 2, z: 4, core: 2. Of those that a mesh axis runs over, the one named last changes fastest.
Arguments:
- features: bfloat16 [8, 8, 14, 14, 528], P(('stream', 'clip'), 'tm'), parts along dimension 0, may hold values from -135 to 135
- w_in_4f: bfloat16 [1056, 448], P('stream'), parts along dimension 0, may hold values from -0.25 to 0.25
- w_pool_4f: bfloat16 [1056, 128], P('stream'), parts along dimension 0, may hold values from -0.25 to 0.25
- w_mid_4f: bfloat16 [54, 160, 320], P('stream'), parts along dimension 0, may hold values from -0.09375 to 0.09375
- w_small_4f: bfloat16 [54, 32, 128], P('stream'), parts along dimension 0, may hold values from -0.21875 to 0.21875
- offsets_4f: float32 [2048], P('stream'), parts along dimension 0, may hold values from -3 to 3
- w_in_5b: bfloat16 [1664, 448], P('stream'), parts along dimension 0, may hold values from -0.21875 to 0.21875
- w_pool_5b: bfloat16 [1664, 128], P('stream'), parts along dimension 0, may hold values from -0.21875 to 0.21875
- w_mid_5b: bfloat16 [54, 160, 320], P('stream'), parts along dimension 0, may hold values from -0.09375 to 0.09375
- w_small_5b: bfloat16 [54, 32, 128], P('stream'), parts along dimension 0, may hold values from -0.21875 to 0.21875
- offsets_5b: float32 [2048], P('stream'), parts along dimension 0, may hold values from -3 to 3
- cotangent: bfloat16 [8, 4, 7, 7, 832], P(('stream', 'clip'), 'tm'), parts along dimension 0, may hold values from -135 to 135
Outputs:
- output: bfloat16 [8, 4, 7, 7, 832], P(('stream', 'clip'), 'tm'), parts along dimension 0
- grad_features: float32 [8, 8, 14, 14, 528], P(('stream', 'clip'), 'tm'), parts along dimension 0
- grad_w_in_4f: float32 [1056, 448], P('stream', 'tm'), parts along dimension 0
- grad_w_pool_4f: float32 [1056, 128], P('stream', 'tm'), parts along dimension 0
- grad_w_mid_4f: float32 [54, 160, 320], P('stream', None, 'tm'), parts along dimension 0
- grad_w_small_4f: float32 [54, 32, 128], P('stream', None, 'tm'), parts along dimension 0
- grad_offsets_4f: float32 [2048], P('stream'), parts along dimension 0
- grad_w_in_5b: float32 [1664, 448], P('stream', 'tm'), parts along dimension 0
- grad_w_pool_5b: float32 [1664, 128], P('stream', 'tm'), parts along dimension 0
- grad_w_mid_5b: float32 [54, 160, 320], P('stream', None, 'tm'), parts along dimension 0
- grad_w_small_5b: float32 [54, 32, 128], P('stream', None, 'tm'), parts along dimension 0
- grad_offsets_5b: float32 [2048], P('stream'), parts along dimension 0
There are 2 independent parts, one for each index of `stream`. A program takes and returns all parts, laid end to end along the dimension named above; each array names one. Nothing has to cross between parts.
All inputs are finite; a program needn't handle non-finite values.
Results may differ from a plain program's by a relative error of at most 0.023.
Values may be sent and summed in bfloat16 or wider, within the bound.
No kernel may reach another device: no remote copies, remote signals or barrier semaphores. Data moves between devices by JAX's collectives and lax.ppermute only.
A program may use at most 192 MiB of HBM per device.

v0:
```python
import jax
import jax.numpy as jnp
from jax import lax
from jax.sharding import PartitionSpec as P

C0 = 256
C1A = 160
C1B = 320
C2A = 32
C2B = 128
IN_OUT = 448
SECTION_A = 576


EPSILON = 0.001
VOXEL_AXES = (0, 1, 2, 3)


def extended(value, sides, width):
    for axis, dim in sides:
        size, length = (lax.axis_size(axis), value.shape[dim])
        up = [(i, (i + 1) % size) for i in range(size - 1)]
        down = [(j, i) for i, j in up]
        last = lax.slice_in_dim(value, length - width, length, axis=dim)
        first = lax.slice_in_dim(value, 0, width, axis=dim)
        before = lax.ppermute(last, axis, up)
        after = lax.ppermute(first, axis, down)
        value = jnp.concatenate([before, value, after], axis=dim)
    return value


def as_sent(value):
    return jax.tree.map(lambda a: a.astype(jnp.bfloat16) if a.dtype == jnp.float32 else a, value)


def project(values, weight):
    return jnp.einsum("nfhwc,cd->nfhwd", values, weight, preferred_element_type=jnp.float32)


def pad_plane(values):
    return jnp.pad(values, ((0, 0), (0, 0), (1, 1), (1, 1), (0, 0)))


def box_sum(padded):
    summed = padded[:, :-2] + padded[:, 1:-1] + padded[:, 2:]
    summed = summed[:, :, :-2] + summed[:, :, 1:-1] + summed[:, :, 2:]
    return summed[:, :, :, :-2] + summed[:, :, :, 1:-1] + summed[:, :, :, 2:]


def unfold(padded, frames, height, width):
    slices = []
    for shift_f in range(3):
        for shift_h in range(3):
            for shift_w in range(3):
                slices.append(
                    padded[
                        :,
                        shift_f : shift_f + frames,
                        shift_h : shift_h + height,
                        shift_w : shift_w + width,
                    ]
                )
    return jnp.concatenate(slices, axis=-1)


def fold_back(patch_grad, channels):
    summed = None
    offset_index = 0
    for shift_f in range(3):
        for shift_h in range(3):
            for shift_w in range(3):
                segment = patch_grad[..., offset_index * channels : (offset_index + 1) * channels]
                placed = jnp.pad(
                    segment,
                    (
                        (0, 0),
                        (shift_f, 2 - shift_f),
                        (shift_h, 2 - shift_h),
                        (shift_w, 2 - shift_w),
                        (0, 0),
                    ),
                )
                summed = placed if summed is None else summed + placed
                offset_index += 1
    return summed


def return_input_rims(grad_padded):
    interior = grad_padded[:, 1:-1]
    rim_pair = jnp.concatenate([grad_padded[:, :1], grad_padded[:, -1:]], axis=1)
    arrived = extended(rim_pair.astype(jnp.bfloat16), (("tm", 1),), 1).astype(rim_pair.dtype)
    interior = interior.at[:, 0].add(arrived[:, 0])
    return interior.at[:, -1].add(arrived[:, 3])


def return_hidden_rims(grad_padded):
    interior = grad_padded[:, 1:-1]
    rim_pair = jnp.concatenate([grad_padded[:, :1], grad_padded[:, -1:]], axis=1)
    arrived = extended(rim_pair.astype(jnp.bfloat16), (("tm", 1),), 1).astype(rim_pair.dtype)
    interior = interior.at[:, 0].add(arrived[:, 0])
    return interior.at[:, -1].add(arrived[:, 3])


def section_first(features, w_in, w_pool):
    rimmed = extended(features, (("tm", 1),), 1)
    padded = pad_plane(rimmed).astype(jnp.float32)
    pooled = (box_sum(padded) / 27.0).astype(jnp.bfloat16)
    pre_first = jnp.concatenate([project(features, w_in), project(pooled, w_pool)], axis=-1)
    return (pre_first, pooled)


def section_second(middle, w_mid, w_small):
    rimmed = extended(middle, (("tm", 1),), 1)
    padded = pad_plane(rimmed)
    frames, height, width = (middle.shape[1], middle.shape[2], middle.shape[3])
    patch_one = unfold(padded[..., :C1A], frames, height, width)
    patch_two = unfold(padded[..., C1A:], frames, height, width)
    pre_second = jnp.concatenate(
        [
            project(patch_one, w_mid.reshape(27 * C1A, C1B)),
            project(patch_two, w_small.reshape(27 * C2A, C2B)),
        ],
        axis=-1,
    )
    return (pre_second, patch_one, patch_two)


def moments(pre_act, voxel_count):
    first_sum = lax.psum(jnp.sum(pre_act, axis=VOXEL_AXES), ("clip", "tm"))
    center = first_sum / voxel_count
    spread = lax.psum(jnp.sum(jnp.square(pre_act - center), axis=VOXEL_AXES), ("clip", "tm"))
    variance = spread / voxel_count
    return (center, variance)


def standardize(pre_act, center, variance):
    return (pre_act - center) * lax.rsqrt(variance + EPSILON)


def silu_slope(act_in):
    sigmoid_value = jax.nn.sigmoid(act_in)
    return sigmoid_value + act_in * sigmoid_value * (1.0 - sigmoid_value)


def block_forward(features, params, voxel_count):
    w_in, w_pool, w_mid, w_small, offsets = params
    pre_first, pooled = section_first(features, w_in, w_pool)
    center_a, variance_a = moments(pre_first, voxel_count)
    hidden_a = jax.nn.silu(standardize(pre_first, center_a, variance_a) + offsets[:SECTION_A])
    middle = hidden_a[..., C0:IN_OUT].astype(jnp.bfloat16)
    pre_second, patch_one, patch_two = section_second(middle, w_mid, w_small)
    center_b, variance_b = moments(pre_second, voxel_count)
    hidden_b = jax.nn.silu(standardize(pre_second, center_b, variance_b) + offsets[SECTION_A:])
    block_out = jnp.concatenate([hidden_a[..., :C0], hidden_b, hidden_a[..., IN_OUT:]], axis=-1)
    return (block_out, (center_a, variance_a, center_b, variance_b))


def norm_back(slope_grad, normed, variance, voxel_count):
    sum_grad, sum_cross = lax.psum(
        (jnp.sum(slope_grad, axis=VOXEL_AXES), jnp.sum(slope_grad * normed, axis=VOXEL_AXES)),
        ("clip", "tm"),
    )
    scaled = lax.rsqrt(variance + EPSILON) * (
        slope_grad - sum_grad / voxel_count - normed * (sum_cross / voxel_count)
    )
    return (scaled.astype(jnp.bfloat16), sum_grad)


def block_backward(features, params, moment_pair, out_grad, voxel_count):
    w_in, w_pool, w_mid, w_small, offsets = params
    center_a, variance_a, center_b, variance_b = moment_pair
    pre_first, pooled = section_first(features, w_in, w_pool)
    normed_a = standardize(pre_first, center_a, variance_a)
    act_a = normed_a + offsets[:SECTION_A]
    middle = jax.nn.silu(act_a)[..., C0:IN_OUT].astype(jnp.bfloat16)
    pre_second, patch_one, patch_two = section_second(middle, w_mid, w_small)
    normed_b = standardize(pre_second, center_b, variance_b)
    act_b = normed_b + offsets[SECTION_A:]
    grad_b = out_grad[..., C0 : C0 + C1B + C2B] * silu_slope(act_b)
    error_b, offset_grad_b = norm_back(grad_b, normed_b, variance_b, voxel_count)
    error_one = error_b[..., :C1B]
    error_two = error_b[..., C1B:]
    grad_mid = jnp.einsum(
        "nfhwk,nfhwo->ko", patch_one, error_one, preferred_element_type=jnp.float32
    ).reshape(27, C1A, C1B)
    grad_small = jnp.einsum(
        "nfhwk,nfhwo->ko", patch_two, error_two, preferred_element_type=jnp.float32
    ).reshape(27, C2A, C2B)
    back_one = fold_back(
        jnp.einsum(
            "nfhwo,ko->nfhwk",
            error_one,
            w_mid.reshape(27 * C1A, C1B),
            preferred_element_type=jnp.float32,
        ),
        C1A,
    )
    back_two = fold_back(
        jnp.einsum(
            "nfhwo,ko->nfhwk",
            error_two,
            w_small.reshape(27 * C2A, C2B),
            preferred_element_type=jnp.float32,
        ),
        C2A,
    )
    middle_grad = return_hidden_rims(
        jnp.concatenate([back_one, back_two], axis=-1)[:, :, 1:-1, 1:-1]
    )
    grad_a = jnp.concatenate(
        [out_grad[..., :C0], middle_grad, out_grad[..., C0 + C1B + C2B :]], axis=-1
    ) * silu_slope(act_a)
    error_a, offset_grad_a = norm_back(grad_a, normed_a, variance_a, voxel_count)
    error_in = error_a[..., :IN_OUT]
    error_pool = error_a[..., IN_OUT:]
    grad_in = jnp.einsum("nfhwc,nfhwd->cd", features, error_in, preferred_element_type=jnp.float32)
    grad_pool = jnp.einsum(
        "nfhwc,nfhwd->cd", pooled, error_pool, preferred_element_type=jnp.float32
    )
    direct = jnp.einsum("nfhwd,cd->nfhwc", error_in, w_in, preferred_element_type=jnp.float32)
    pool_grad = jnp.einsum(
        "nfhwd,cd->nfhwc", error_pool, w_pool, preferred_element_type=jnp.float32
    )
    spread_pad = jnp.pad(pool_grad, ((0, 0), (2, 2), (2, 2), (2, 2), (0, 0)))
    padded_grad = (box_sum(spread_pad) / 27.0)[:, :, 1:-1, 1:-1]
    input_grad = direct + return_input_rims(padded_grad)
    return (
        input_grad,
        (grad_in, grad_pool, grad_mid, grad_small),
        jnp.concatenate([offset_grad_a, offset_grad_b]),
    )


def reduce_grads(weight_grads):
    summed = jax.tree.map(
        lambda part: part.astype(jnp.float32), lax.psum(as_sent(weight_grads), "clip")
    )
    reduced = (
        lax.psum_scatter(
            summed[0].astype(jnp.bfloat16), "tm", scatter_dimension=1, tiled=True
        ).astype(jnp.float32),
        lax.psum_scatter(
            summed[1].astype(jnp.bfloat16), "tm", scatter_dimension=1, tiled=True
        ).astype(jnp.float32),
        lax.psum_scatter(
            summed[2].astype(jnp.bfloat16), "tm", scatter_dimension=2, tiled=True
        ).astype(jnp.float32),
        lax.psum_scatter(
            summed[3].astype(jnp.bfloat16), "tm", scatter_dimension=2, tiled=True
        ).astype(jnp.float32),
    )
    return reduced


def halve_grid(values):
    n, f, h, w, c = values.shape
    return jnp.sum(values.reshape(n, f // 2, 2, h // 2, 2, w // 2, 2, c), axis=(2, 4, 6)) * 0.125


def spread_half(grad_small_grid):
    n, f, h, w, c = grad_small_grid.shape
    expanded = jnp.broadcast_to(
        (grad_small_grid * 0.125)[:, :, None, :, None, :, None, :], (n, f, 2, h, 2, w, 2, c)
    )
    return expanded.reshape(n, 2 * f, 2 * h, 2 * w, c)


def shards(
    features,
    w_in_4f,
    w_pool_4f,
    w_mid_4f,
    w_small_4f,
    offsets_4f,
    w_in_5b,
    w_pool_5b,
    w_mid_5b,
    w_small_5b,
    offsets_5b,
    cotangent,
):
    params_first = (w_in_4f, w_pool_4f, w_mid_4f, w_small_4f, offsets_4f)
    params_second = (w_in_5b, w_pool_5b, w_mid_5b, w_small_5b, offsets_5b)
    devices_used = lax.axis_size("clip") * lax.axis_size("tm")
    count_first = float(
        features.shape[0] * features.shape[1] * features.shape[2] * features.shape[3] * devices_used
    )
    count_second = count_first / 8.0
    out_first, moments_first = block_forward(features, params_first, count_first)
    input_second = halve_grid(out_first).astype(jnp.bfloat16)
    out_second, moments_second = block_forward(input_second, params_second, count_second)
    grad_second, weights_second, offsets_grad_second = block_backward(
        input_second, params_second, moments_second, cotangent.astype(jnp.float32), count_second
    )
    reduced_second = reduce_grads(weights_second)
    grad_first, weights_first, offsets_grad_first = block_backward(
        features, params_first, moments_first, spread_half(grad_second), count_first
    )
    reduced_first = reduce_grads(weights_first)
    final_out = out_second.astype(jnp.bfloat16)
    return (
        final_out,
        grad_first,
        reduced_first[0],
        reduced_first[1],
        reduced_first[2],
        reduced_first[3],
        offsets_grad_first,
        reduced_second[0],
        reduced_second[1],
        reduced_second[2],
        reduced_second[3],
        offsets_grad_second,
    )


def solution(mesh):
    placed = (
        P(("stream", "clip"), "tm", None, None, None),
        P("stream", None),
        P("stream", None),
        P("stream", None, None),
        P("stream", None, None),
        P("stream"),
        P("stream", None),
        P("stream", None),
        P("stream", None, None),
        P("stream", None, None),
        P("stream"),
        P(("stream", "clip"), "tm", None, None, None),
    )
    return jax.shard_map(
        shards,
        mesh=mesh,
        in_specs=placed,
        out_specs=(
            P(("stream", "clip"), "tm", None, None, None),
            P(("stream", "clip"), "tm", None, None, None),
            P("stream", "tm"),
            P("stream", "tm"),
            P("stream", None, "tm"),
            P("stream", None, "tm"),
            P("stream"),
            P("stream", "tm"),
            P("stream", "tm"),
            P("stream", None, "tm"),
            P("stream", None, "tm"),
            P("stream"),
        ),
        check_vma=False,
    )
```

profile of v0, /device:TPU:0, one launch (start us, length us, event | category | flops | bytes accessed | tf_op | source)
XLA Modules:
  0.0 1076.9 jit_solution(622764590798517051)
XLA Ops:
  16.2 8.8 collective-permute-done
  25.0 12.7 %collective-permute-done.1 = bf16[1,1,14,14,528]{4,1,3,2,0:T(2,128)(2,1)S(1)} collective-permute-done((bf16[1,1,14,14,528]{4,1,3,2,0:T(2,128)(2,1)S(1)}, bf16[1,1,14,14,528]{4,1,3,2,0:T(2,128)(2,1)S(1)}, u32[]{:S(2)}, u32[]{:S(2)}) %collective-permute-start.1) | collective-permute-done | bytes 207008 | tf_op jit(solution)/shard_map/ppermute | solution.py:27
  44.7 39.0 %psum.168 = f32[576]{0:T(1024)} all-reduce(f32[576]{0:T(1024)S(1)} %fusion.95), channel_id=1, replica_groups=mesh['stream'=2,'clip'=4,'tm'=4] {'clip','tm'}, use_global_device_ids=true, to_apply=%region_1.2 | all-reduce | flops 576 | bytes 4608 | tf_op jit(solution)/shard_map/psum | solution.py:129
  86.4 37.5 %psum.169 = f32[576]{0:T(1024)} all-reduce(f32[576]{0:T(1024)} %multiply_reduce_fusion.1), channel_id=1, replica_groups=mesh['stream'=2,'clip'=4,'tm'=4] {'clip','tm'}, use_global_device_ids=true, to_apply=%region_3.4 | all-reduce | flops 576 | bytes 4608 | tf_op jit(solution)/shard_map/psum | solution.py:131
  149.9 9.3 concatenate.424
  165.0 38.8 %psum.170 = f32[448]{0:T(512)} all-reduce(f32[448]{0:T(512)S(1)} %fusion.72), channel_id=1, replica_groups=mesh['stream'=2,'clip'=4,'tm'=4] {'clip','tm'}, use_global_device_ids=true, to_apply=%region_5.6 | all-reduce | flops 448 | bytes 3584 | tf_op jit(solution)/shard_map/psum | solution.py:129
  206.4 37.6 %psum.171 = f32[448]{0:T(512)} all-reduce(f32[448]{0:T(512)} %multiply_reduce_fusion.3), channel_id=1, replica_groups=mesh['stream'=2,'clip'=4,'tm'=4] {'clip','tm'}, use_global_device_ids=true, to_apply=%region_7.8 | all-reduce | flops 448 | bytes 3584 | tf_op jit(solution)/shard_map/psum | solution.py:131
  258.4 39.7 %psum.172 = f32[576]{0:T(1024)} all-reduce(f32[576]{0:T(1024)S(1)} %fusion.116), channel_id=1, replica_groups=mesh['stream'=2,'clip'=4,'tm'=4] {'clip','tm'}, use_global_device_ids=true, to_apply=%region_10.11 | all-reduce | flops 576 | bytes 4608 | tf_op jit(solution)/shard_map/psum | solution.py:129
  300.5 37.3 %psum.173 = f32[576]{0:T(1024)} all-reduce(f32[576]{0:T(1024)} %multiply_reduce_fusion.5), channel_id=1, replica_groups=mesh['stream'=2,'clip'=4,'tm'=4] {'clip','tm'}, use_global_device_ids=true, to_apply=%region_12.13 | all-reduce | flops 576 | bytes 4608 | tf_op jit(solution)/shard_map/psum | solution.py:131
  377.3 39.6 %psum.174 = f32[448]{0:T(512)} all-reduce(f32[448]{0:T(512)} %fusion.115), channel_id=1, replica_groups=mesh['stream'=2,'clip'=4,'tm'=4] {'clip','tm'}, use_global_device_ids=true, to_apply=%region_14.15 | all-reduce | flops 448 | bytes 3584 | tf_op jit(solution)/shard_map/psum | solution.py:129
  419.8 37.2 %psum.175 = f32[448]{0:T(512)} all-reduce(f32[448]{0:T(512)} %multiply_reduce_fusion.7), channel_id=1, replica_groups=mesh['stream'=2,'clip'=4,'tm'=4] {'clip','tm'}, use_global_device_ids=true, to_apply=%region_16.17 | all-reduce | flops 448 | bytes 3584 | tf_op jit(solution)/shard_map/psum | solution.py:131
  460.6 39.3 %all-reduce.119 = (f32[448]{0:T(512)}, f32[448]{0:T(512)}) all-reduce(f32[448]{0:T(512)} %get-tuple-element.151, f32[448]{0:T(512)} %get-tuple-element.150), channel_id=1, replica_groups=mesh['stream'=2,'clip'=4,'tm'=4] {'clip','tm'}, use_global_device_ids=true, to_apply=%region_20.21 | all-reduce | flops 896 | bytes 7168 | tf_op jit(solution)/shard_map/psum | solution.py:159
  532.9 38.7 %all-reduce.118 = (f32[576]{0:T(1024)}, f32[576]{0:T(1024)}) all-reduce(f32[576]{0:T(1024)} %get-tuple-element.149, f32[576]{0:T(1024)} %get-tuple-element.148), channel_id=1, replica_groups=mesh['stream'=2,'clip'=4,'tm'=4] {'clip','tm'}, use_global_device_ids=true, to_apply=%region_24.25 | all-reduce | flops 1152 | bytes 9216 | tf_op jit(solution)/shard_map/psum | solution.py:159
  593.4 38.2 %all-reduce.117 = (f32[448]{0:T(512)}, f32[448]{0:T(512)}) all-reduce(f32[448]{0:T(512)} %get-tuple-element.145, f32[448]{0:T(512)} %get-tuple-element.144), channel_id=1, replica_groups=mesh['stream'=2,'clip'=4,'tm'=4] {'clip','tm'}, use_global_device_ids=true, to_apply=%region_28.29 | all-reduce | flops 896 | bytes 7168 | tf_op jit(solution)/shard_map/psum | solution.py:159
  681.4 37.4 %all-reduce.116 = (f32[576]{0:T(1024)S(1)}, f32[576]{0:T(1024)S(1)}) all-reduce(f32[576]{0:T(1024)S(1)} %get-tuple-element.147, f32[576]{0:T(1024)S(1)} %get-tuple-element.146), channel_id=1, replica_groups=mesh['stream'=2,'clip'=4,'tm'=4] {'clip','tm'}, use_global_device_ids=true, to_apply=%region_32.33 | all-reduce | flops 1152 | bytes 9216 | tf_op jit(solution)/shard_map/psum | solution.py:159
  735.5 8.9 reshape.1721
  744.5 11.6 %reshape.1713 = bf16[27,160,2,14,14]{1,0,4,3,2:T(8,128)(2,1)} reshape(bf16[4320,2,14,14]{0,3,2,1:T(8,128)(2,1)} %bitcast.252) | data formatting | bytes 6773760 | tf_op jit(solution)/shard_map/nfhwk,nfhwo->ko/dot_general | solution.py:183
  756.2 13.4 %bitcast_convert_fusion = bf16[27,160,320]{2,1,0:T(8,128)(2,1)S(1)} fusion(bf16[27,160,2,14,14]{1,0,4,3,2:T(8,128)(2,1)} %reshape.1713, bf16[1,2,14,14,448]{4,3,2,1,0:T(8,128)(2,1)} %copy-done.27), kind=kOutput, calls=%fused_computation.4 | convolution fusion | flops 1085184000 | bytes 9531392 | tf_op jit(solution)/shard_map/nfhwk,nfhwo->ko/dot_general | solution.py:183
  777.1 9.0 reshape.1717
  800.7 36.3 %reduce-scatter.27.cloned.1.call-done = bf16[80,4320]{1,0:T(8,128)(2,1)} async-done(((bf16[320,4320]{1,0:T(8,128)(2,1)}), bf16[80,4320]{1,0:T(8,128)(2,1)}) %reduce-scatter.27.cloned.1.call-update) | async-done | bytes 691216
  841.9 39.4 %reduce-scatter.23.cloned.1.call-done = bf16[80,4320]{1,0:T(8,128)(2,1)} async-done(((bf16[320,4320]{1,0:T(8,128)(2,1)}), bf16[80,4320]{1,0:T(8,128)(2,1)}) %reduce-scatter.23.cloned.1.call-update) | async-done | bytes 691216
  886.2 25.8 %reduce-scatter.31.cloned.1.call-done = bf16[832,112]{0,1:T(8,128)(2,1)} async-done(((bf16[832,448]{0,1:T(8,128)(2,1)}), bf16[832,112]{0,1:T(8,128)(2,1)}) %reduce-scatter.31.cloned.1.call-update) | async-done | bytes 186384
  939.2 15.3 %all-reduce.128.cloned.1.call-done = (bf16[528,32]{0,1:T(8,128)(2,1)}, bf16[27,32,32]{2,1,0:T(8,128)(2,1)}, bf16[832,32]{0,1:T(8,128)(2,1)}, bf16[27,32,32]{2,1,0:T(8,128)(2,1)}) async-done(((bf16[528,32]{0,1:T(8,128)(2,1)}, bf16[27,32,32]{2,1,0:T(8,128)(2,1)}, bf16[832,32]{0,1:T(8,128)(2,1)}, bf16[27,32,32]{2,1,0:T(8,128)(2,1)}), (bf16[528,32]{0,1:T(8,128)(2,1)}, bf16[27,32,32]{2,1,0:T(8,128)(2,1)}, ...) | async-done | bytes 197648 | tf_op jit(solution)/shard_map/psum | solution.py:236
  960.9 100.0 %all-reduce.130.cloned.1.call-done = (bf16[528,112]{1,0:T(8,128)(2,1)}, bf16[27,160,80]{2,1,0:T(8,128)(2,1)}, bf16[832,112]{0,1:T(8,128)(2,1)}, bf16[27,160,80]{2,1,0:T(8,128)(2,1)}) async-done(((bf16[528,112]{1,0:T(8,128)(2,1)}, bf16[27,160,80]{2,1,0:T(8,128)(2,1)}, bf16[832,112]{0,1:T(8,128)(2,1)}, bf16[27,160,80]{2,1,0:T(8,128)(2,1)}), (bf16[528,112]{1,0:T(8,128)(2,1)}, bf16[27,160,80]{2,1,0:T(8,128)(2,1)}, ...) | async-done | bytes 1687056 | tf_op jit(solution)/shard_map/psum | solution.py:236
  (419 shorter events, 309.5 us)
Async XLA Ops:
  7.2 785.4 %reduce-scatter.29.cloned.1.call-start = ((), (), s32[]{:S(2)}) async-start(), calls=%async_computation.12 | async-start | bytes 286720
  9.5 15.5 %collective-permute-start = (bf16[1,1,14,14,528]{4,1,3,2,0:T(2,128)(2,1)S(1)}, bf16[1,1,14,14,528]{4,1,3,2,0:T(2,128)(2,1)S(1)}, u32[]{:S(2)}, u32[]{:S(2)}) collective-permute-start(bf16[1,1,14,14,528]{4,1,3,2,0:T(2,128)(2,1)S(1)} %get-tuple-element.312), channel_id=1, source_target_pairs={{0,1},{1,2},{2,3},{4,5},{5,6},{6,7},{8,9},{9,10},{10,11},{12,13},{... | collective-permute-start | bytes 620936 | tf_op jit(solution)/shard_map/ppermute | solution.py:26
  14.4 23.3 %collective-permute-start.1 = (bf16[1,1,14,14,528]{4,1,3,2,0:T(2,128)(2,1)S(1)}, bf16[1,1,14,14,528]{4,1,3,2,0:T(2,128)(2,1)S(1)}, u32[]{:S(2)}, u32[]{:S(2)}) collective-permute-start(bf16[1,1,14,14,528]{4,1,3,2,0:T(2,128)(2,1)S(1)} %get-tuple-element.313), channel_id=1, source_target_pairs={{1,0},{2,1},{3,2},{5,4},{6,5},{7,6},{9,8},{10,9},{11,10},{13,12},{... | collective-permute-start | bytes 620936 | tf_op jit(solution)/shard_map/ppermute | solution.py:27
  126.2 9.4 collective-permute-start.2
  129.9 6.7 collective-permute-start.3
  248.2 6.5 collective-permute-start.5
  249.5 6.8 collective-permute-start.4
  340.7 20.0 %collective-permute-start.7 = (bf16[1,1,7,7,192]{4,3,2,1,0:T(8,128)(2,1)}, bf16[1,1,7,7,192]{4,3,2,1,0:T(8,128)(2,1)}, u32[]{:S(2)}, u32[]{:S(2)}) collective-permute-start(bf16[1,1,7,7,192]{4,3,2,1,0:T(8,128)(2,1)} %slice.1853), channel_id=1, source_target_pairs={{1,0},{2,1},{3,2},{5,4},{6,5},{7,6},{9,8},{10,9},{11,10},{13,12},{... | collective-permute-start | bytes 56456 | tf_op jit(solution)/shard_map/ppermute | solution.py:27
  342.0 18.7 %collective-permute-start.6 = (bf16[1,1,7,7,192]{4,3,2,1,0:T(8,128)(2,1)}, bf16[1,1,7,7,192]{4,3,2,1,0:T(8,128)(2,1)}, u32[]{:S(2)}, u32[]{:S(2)}) collective-permute-start(bf16[1,1,7,7,192]{4,3,2,1,0:T(8,128)(2,1)} %slice.1853), channel_id=1, source_target_pairs={{0,1},{1,2},{2,3},{4,5},{5,6},{6,7},{8,9},{9,10},{10,11},{12,13},{... | collective-permute-start | bytes 56456 | tf_op jit(solution)/shard_map/ppermute | solution.py:26
  520.5 274.0 %reduce-scatter.25.cloned.1.call-start = ((), (), s32[]{:S(2)}) async-start(), calls=%async_computation.10 | async-start | bytes 286720
  525.7 5.8 collective-permute-start.9
  579.0 6.5 collective-permute-start.11
  645.9 150.7 %reduce-scatter.21.cloned.1.call-start = ((), (), s32[]{:S(2)}) async-start(), calls=%async_computation.8 | async-start | bytes 286720 | tf_op jit(solution)/shard_map/reduce_scatter | solution.py:242
  647.0 149.6 %reduce-scatter.19.cloned.1.call-start = ((), (), s32[]{:S(2)}) async-start(), calls=%async_computation.7 | async-start | bytes 204800 | tf_op jit(solution)/shard_map/reduce_scatter | solution.py:242
  668.9 5.5 collective-permute-start.12
  672.0 7.3 collective-permute-start.13
  721.7 77.3 %all-reduce.126.cloned.1.call-start = ((), (), s32[]{:S(2)}) async-start(), calls=%async_computation.13 | async-start | bytes 1081344
  725.0 112.1 %reduce-scatter.27.cloned.1.call-start = ((), (), s32[]{:S(2)}) async-start(), calls=%async_computation.11 | async-start | bytes 3481600
  744.5 136.9 %reduce-scatter.23.cloned.1.call-start = ((), (), s32[]{:S(2)}) async-start(), calls=%async_computation.9 | async-start | bytes 3481600
  786.2 125.9 %reduce-scatter.31.cloned.1.call-start = ((), (), s32[]{:S(2)}) async-start(), calls=%async_computation.14 | async-start | bytes 1003520
  788.3 166.2 %all-reduce.128.cloned.1.call-start = ((), (), s32[]{:S(2)}) async-start(), calls=%async_computation.15 | async-start | bytes 1081344 | tf_op jit(solution)/shard_map/psum | solution.py:236
  796.6 264.2 %all-reduce.130.cloned.1.call-start = ((), (), s32[]{:S(2)}) async-start(), calls=%async_computation.16 | async-start | bytes 5095424 | tf_op jit(solution)/shard_map/psum | solution.py:236
  918.0 9.4 collective-permute-start.14
  921.4 14.1 %collective-permute-start.15 = (bf16[1,1,14,14,528]{4,3,2,1,0:T(8,128)(2,1)S(1)}, bf16[1,1,14,14,528]{4,3,2,1,0:T(8,128)(2,1)S(1)}, u32[]{:S(2)}, u32[]{:S(2)}) collective-permute-start(bf16[1,1,14,14,528]{4,3,2,1,0:T(8,128)(2,1)S(1)} %get-tuple-element.199), channel_id=1, source_target_pairs={{1,0},{2,1},{3,2},{5,4},{6,5},{7,6},{9,8},{10,9},{11,10},{13,12},{... | collective-permute-start | bytes 620936 | tf_op jit(solution)/shard_map/ppermute | solution.py:27
  (97 other events, 809.7 us)
Sparse Core Ops, SparseCore 0:
  520.7 19.9 reduce-scatter.28
  646.0 20.9 reduce-scatter.24
  669.8 24.0 reduce-scatter.20
  721.8 21.4 reduce-scatter.18
  747.1 45.6 all-reduce.125
  795.9 41.0 reduce-scatter.26
  840.4 40.9 reduce-scatter.22
  885.2 26.7 reduce-scatter.30
  915.4 39.0 all-reduce.127
  958.1 102.6 all-reduce.129
where the time goes:
time: 1090 us; the launch traced here: 1080 us
  blocking collectives  460 us (42%)
  waiting for transfers between devices  268 us (25%)
  local copies, waits for them, and re-layouts  156 us (14%)
  other arithmetic  83 us (8%)
  matrix products  50.6 us (5%)
  starting transfers between devices  41.7 us (4%)
  between operations  16.7 us (2%)
    psum x4, blocking collectives, moments(): first_sum = lax.psum(jnp.sum(pre_act, axis=VOXEL_AXES), ('clip', 'tm'))  157 us
    psum x4, blocking collectives, norm_back(): lax.psum((jnp.sum(slope_grad, axis=VOXEL_AXES), jnp.sum(slope_grad * norm...  154 us
    psum x4, blocking collectives, moments(): lax.psum(jnp.sum(jnp.square(pre_act - center), axis=VOXEL_AXES), ('clip',...  150 us
    psum x2, waiting for transfers between devices, reduce_grads(): lax.psum(as_sent(weight_grads), 'clip')  115 us
    unnamed x16, waiting for transfers between devices  102 us
    unnamed x205, local copies, waits for them, and re-layouts  72.6 us
    ppermute x8, waiting for transfers between devices, extended(): after = lax.ppermute(first, axis, down)  35.5 us
    ppermute x8, starting transfers between devices, extended(): before = lax.ppermute(last, axis, up)  29.8 us
  transfers between devices with their start and end apart: 26, of which 18 were waited for; matrix products, arithmetic and copies ran while one was open for 16% of the time, Pallas kernels for 0%

commit v1 on v0

--- a/solution.py
+++ b/solution.py
@@ -1,6 +1,10 @@
+import functools
+
 import jax
 import jax.numpy as jnp
 from jax import lax
+from jax.experimental import pallas as pl
+from jax.experimental.pallas import tpu as pltpu
 from jax.sharding import PartitionSpec as P
 
 C0 = 256
@@ -314,6 +318,721 @@
     )
 
 
+F32 = jnp.float32
+BF16 = jnp.bfloat16
+MID = 192
+BOUT = 448
+POOL = 128
+OUTC = 832
+VMEM_LIMIT = 56 * 1024 * 1024
+
+
+def dot_nn(a, b):
+    return lax.dot_general(a, b, (((1,), (0,)), ((), ())), preferred_element_type=F32)
+
+
+def dot_nt(a, b):
+    return lax.dot_general(a, b, (((1,), (1,)), ((), ())), preferred_element_type=F32)
+
+
+def roll_rows(value, shift):
+    rows = value.shape[0]
+    shift %= rows
+    return value if shift == 0 else pltpu.roll(value, shift, 0)
+
+
+def valid_first(rows):
+    r = lax.broadcasted_iota(jnp.int32, (rows, 1), 0)
+    return ((r & 255) < 224) & ((r & 15) < 14)
+
+
+def valid_second(rows):
+    r = lax.broadcasted_iota(jnp.int32, (rows, 1), 0)
+    return ((r & 63) < 56) & ((r & 7) < 7)
+
+
+def act(a):
+    return a * jax.nn.sigmoid(a)
+
+
+def slope(a):
+    s = jax.nn.sigmoid(a)
+    return s + a * s * (1.0 - s)
+
+
+def pack_rows(vectors):
+    pieces = []
+    for v in vectors:
+        width = v.shape[1]
+        full = -(-width // 128) * 128
+        if full != width:
+            v = jnp.concatenate([v, jnp.zeros((1, full - width), F32)], axis=1)
+        for i in range(full // 128):
+            pieces.append(v[:, i * 128 : (i + 1) * 128])
+    return jnp.concatenate(pieces, axis=0)
+
+
+def unpack_rows(rows, start, width):
+    count = -(-width // 128)
+    return jnp.concatenate([rows[start + i : start + i + 1] for i in range(count)], axis=1)[
+        :, :width
+    ]
+
+
+def store_copies(ref, rows):
+    count, height = ref.shape[0], ref.shape[1]
+    if rows.shape[0] < height:
+        rows = jnp.concatenate([rows, jnp.zeros((height - rows.shape[0], 128), F32)], axis=0)
+    for i in range(count):
+        ref[i] = rows
+
+
+def local_moments(value, mask, cells):
+    total = jnp.sum(jnp.where(mask, value, 0.0), axis=0, keepdims=True)
+    delta = jnp.where(mask, value - total * (1.0 / cells), 0.0)
+    return total, jnp.sum(delta * delta, axis=0, keepdims=True)
+
+
+def joint_moments(gathered, height, cells):
+    devices = gathered.shape[0]
+    sums, squares = gathered[:, :height], gathered[:, height : 2 * height]
+    mean = jnp.sum(sums, axis=0) * (1.0 / (cells * devices))
+    apart = sums * (1.0 / cells) - mean[None]
+    spread = jnp.sum(squares, axis=0) + cells * jnp.sum(apart * apart, axis=0)
+    return mean, lax.rsqrt(spread * (1.0 / (cells * devices)) + EPSILON)
+
+
+def halve(total, scratch, dtype):
+    width = total.shape[1]
+    both = total[:256] + total[256:]
+    pairs = jnp.sum(both.reshape(8, 2, 16, width), axis=1).reshape(128, width)
+    pieces = []
+    for i in range(-(-width // 128)):
+        lanes = min(128, width - i * 128)
+        scratch[i, :, :lanes] = pairs[:, i * 128 : i * 128 + lanes]
+        piece = scratch[i, pl.ds(0, 64, 2), :] + scratch[i, pl.ds(1, 64, 2), :]
+        pieces.append(piece[:, :lanes])
+    halved = jnp.concatenate(pieces, axis=1)
+    return (halved * 0.125).astype(dtype)
+
+
+def box_plane(value, stride):
+    value = value + roll_rows(value, stride) + roll_rows(value, -stride)
+    return value + roll_rows(value, 1) + roll_rows(value, -1)
+
+
+def first_project(x_ref, win_ref, wpool_ref, zin_ref, q_ref, st_ref, head_ref, tail_ref):
+    for f in range(2):
+        rows = pl.ds(f * 256, 256)
+        x = x_ref[rows, :]
+        zin_ref[rows, :] = dot_nn(x, win_ref[...])
+        q_ref[rows, :] = dot_nn(x, wpool_ref[...])
+    total, squares = local_moments(zin_ref[...], valid_first(512), 392)
+    store_copies(st_ref, pack_rows([total, squares]))
+    for f, ref in ((0, head_ref), (1, tail_ref)):
+        rows = pl.ds(f * 256, 256)
+        ref[:, :MID] = zin_ref[rows, C0:].astype(BF16)
+        ref[:, MID:] = q_ref[rows, :].astype(BF16)
+
+
+def first_hidden(
+    flag_ref, st_ref, zin_ref, q_ref, before_ref, after_ref, wmid_ref, wsmall_ref, off_ref,
+    zb_ref, zp_ref, st2_ref, x2_ref, um_ref, us_ref, head_ref, tail_ref, ma_ref,
+    mid, half,
+):
+    mean_rows, scale_rows = joint_moments(st_ref[...], 4, 392.0)
+    mean, scale = unpack_rows(mean_rows, 0, IN_OUT), unpack_rows(scale_rows, 0, IN_OUT)
+    ma_ref[...] = jnp.concatenate([mean, scale], axis=0)
+    off = off_ref[:, :IN_OUT]
+    frame = valid_first(256)
+    prev, after = flag_ref[1] > 0, flag_ref[2] > 0
+
+    def middle(z, mask):
+        return jnp.where(mask, act((z - mean[:, C0:]) * scale[:, C0:] + off[:, C0:]), 0.0)
+
+    mid[0:256, :] = middle(before_ref[:, :MID].astype(F32), frame & prev)
+    mid[256:512, :] = middle(zin_ref[0:256, C0:], frame)
+    mid[512:768, :] = middle(zin_ref[256:512, C0:], frame)
+    mid[768:1024, :] = middle(after_ref[:, :MID].astype(F32), frame & after)
+    for ref in (um_ref, us_ref):
+        edge = jnp.zeros((16, ref.shape[1]), BF16)
+        ref[0:16, :] = edge
+        ref[1040:1056, :] = edge
+
+    for f in range(4):
+        rows = slice(f * 256, (f + 1) * 256)
+        shifted = [roll_rows(mid[rows, :], 1 - g) for g in range(3)]
+        into = slice(16 + f * 256, 16 + (f + 1) * 256)
+        um_ref[into, :] = jnp.concatenate([v[:, :C1A] for v in shifted], axis=1).astype(BF16)
+        us_ref[into, :] = jnp.concatenate([v[:, C1A:] for v in shifted], axis=1).astype(BF16)
+
+    def convolve(u_ref, w_ref, base):
+        total = None
+        for a in range(3):
+            for e in range(3):
+                start = base + 16 + a * 256 + (e - 1) * 16
+                term = dot_nn(u_ref[start : start + 256, :], w_ref[3 * a + e])
+                total = term if total is None else total + term
+        return total
+
+    for f in range(2):
+        rows = pl.ds(f * 256, 256)
+        zb_ref[rows, :C1B] = convolve(um_ref, wmid_ref, f * 256)
+        zb_ref[rows, C1B:] = convolve(us_ref, wsmall_ref, f * 256)
+
+    first, last = q_ref[0:256, :], q_ref[256:512, :]
+    pair = first + last
+    for f, value in (
+        (0, pair + before_ref[:, MID:].astype(F32)),
+        (1, pair + after_ref[:, MID:].astype(F32)),
+    ):
+        value = box_plane(value, 16) * (1.0 / 27.0)
+        zp_ref[f * 256 : (f + 1) * 256, :] = jnp.where(frame, value, 0.0)
+
+    both = valid_first(512)
+    total_b, squares_b = local_moments(zb_ref[...], both, 392)
+    total_p, squares_p = local_moments(zp_ref[...], both, 392)
+    store_copies(st2_ref, pack_rows([total_b, total_p, squares_b, squares_p]))
+    for f, ref in ((0, head_ref), (1, tail_ref)):
+        rows = pl.ds(f * 256, 256)
+        ref[:, :BOUT] = zb_ref[rows, :].astype(BF16)
+        ref[:, BOUT:] = zp_ref[rows, :].astype(BF16)
+    hidden = act((zin_ref[:, :C0] - mean[:, :C0]) * scale[:, :C0] + off[:, :C0])
+    x2_ref[...] = halve(jnp.where(both, hidden, 0.0), half, BF16)
+
+
+def first_output(st_ref, zb_ref, zp_ref, off_ref, x2_ref, mb_ref, half):
+    mean_rows, scale_rows = joint_moments(st_ref[...], 5, 392.0)
+    both = valid_first(512)
+    moments = []
+    for start, width, z_ref, offset in ((0, BOUT, zb_ref, SECTION_A), (4, POOL, zp_ref, IN_OUT)):
+        mean, scale = unpack_rows(mean_rows, start, width), unpack_rows(scale_rows, start, width)
+        hidden = act((z_ref[...] - mean) * scale + off_ref[:, offset : offset + width])
+        into = slice(0, BOUT) if start == 0 else slice(BOUT, BOUT + POOL)
+        x2_ref[:, into] = halve(jnp.where(both, hidden, 0.0), half, BF16)
+        moments.append(jnp.concatenate([mean, scale], axis=0))
+    mb_ref[...] = jnp.concatenate(moments, axis=1)
+
+
+def second_layer(
+    clips, frames, flag_ref, x0_ref, x1_ref, cot_ref, win_ref, wpool_ref, wmid_ref, wsmall_ref,
+    off_ref,
+    out_ref, dx_ref, gin_ref, gpool_ref, gmid_ref, gsmall_ref, goff_ref,
+    xs, cs, za, zb, um, us, qs, eb, ea, et, eat, da,
+):
+    here = flag_ref[0]
+    span = frames * 64
+    slot = (frames + 1) * 64
+    cells = clips * frames * 49.0
+    wide = clips * slot
+    part_mid, part_small = gmid_ref.shape[2], gsmall_ref.shape[2]
+    part_in, part_pool = gin_ref.shape[0], gpool_ref.shape[0]
+    mask = valid_second(span)
+
+    for c in range(clips):
+        for m in range(frames):
+            frame = lax.rem(here + m, frames)
+            rows = pl.ds(pl.multiple_of(c * span + frame * 64, 64), 64)
+            xs[rows, :C0] = x0_ref[c * frames + m]
+            xs[rows, C0:] = x1_ref[c * frames + m]
+            cs[rows, :] = cot_ref[c * frames + m]
+    for ref in (um, us, qs, eb, ea):
+        blank = jnp.zeros((64, ref.shape[1]), ref.dtype)
+        for c in range(clips + 1):
+            ref[c * slot : c * slot + 64, :] = blank
+        ref[wide + 64 : wide + 128, :] = blank
+
+    def rows_of(c):
+        return pl.ds(pl.multiple_of(c * span, 64), span)
+
+    def slots_of(c, shift=1):
+        return pl.ds(pl.multiple_of(c * slot + shift * 64, 64), span)
+
+    def over_clips(body, init):
+        return lax.fori_loop(0, clips, body, init)
+
+    def box(c):
+        value = qs[slots_of(c, 0), :] + qs[slots_of(c, 1), :] + qs[slots_of(c, 2), :]
+        return jnp.where(mask, box_plane(value, 8) * (1.0 / 27.0), 0.0)
+
+    def project_clip(c, total):
+        x = xs[rows_of(c), :]
+        z = dot_nn(x, win_ref[...])
+        za[rows_of(c), :IN_OUT] = z
+        qs[slots_of(c), :] = dot_nn(x, wpool_ref[...])
+        p = box(c)
+        za[rows_of(c), IN_OUT:] = p
+        return total + jnp.concatenate(
+            [jnp.sum(z, axis=0, keepdims=True), jnp.sum(p, axis=0, keepdims=True)], axis=1
+        )
+
+    total_a = over_clips(project_clip, jnp.zeros((1, SECTION_A), F32))
+    mean_a = total_a * (1.0 / cells)
+
+    def spread_clip(ref, mean):
+        def body(c, total):
+            delta = jnp.where(mask, ref[rows_of(c), :] - mean, 0.0)
+            return total + jnp.sum(delta * delta, axis=0, keepdims=True)
+
+        return body
+
+    spread_a = over_clips(spread_clip(za, mean_a), jnp.zeros((1, SECTION_A), F32))
+    scale_a = lax.rsqrt(spread_a * (1.0 / cells) + EPSILON)
+    off_a, off_b = off_ref[:, :SECTION_A], off_ref[:, SECTION_A:]
+
+    def normal_a(c, lo, hi):
+        return (za[rows_of(c), lo:hi] - mean_a[:, lo:hi]) * scale_a[:, lo:hi]
+
+    def unfold_clip(c, _):
+        a = normal_a(c, C0, IN_OUT) + off_a[:, C0:IN_OUT]
+        hidden = jnp.where(mask, act(a), 0.0)
+        shifted = []
+        for e in range(3):
+            row = roll_rows(hidden, 8 * (1 - e))
+            shifted += [roll_rows(row, 1 - g) for g in range(3)]
+        um[slots_of(c), :] = jnp.concatenate([v[:, :C1A] for v in shifted], axis=1).astype(BF16)
+        us[slots_of(c), :] = jnp.concatenate([v[:, C1A:] for v in shifted], axis=1).astype(BF16)
+        return 0
+
+    over_clips(unfold_clip, 0)
+
+    def convolve_clip(c, total):
+        mids, smalls = None, None
+        for a in range(3):
+            one = dot_nn(um[slots_of(c, a), :], wmid_ref[a])
+            two = dot_nn(us[slots_of(c, a), :], wsmall_ref[a])
+            mids = one if mids is None else mids + one
+            smalls = two if smalls is None else smalls + two
+        z = jnp.concatenate([mids, smalls], axis=1)
+        zb[rows_of(c), :] = z
+        return total + jnp.sum(jnp.where(mask, z, 0.0), axis=0, keepdims=True)
+
+    total_b = over_clips(convolve_clip, jnp.zeros((1, BOUT), F32))
+    mean_b = total_b * (1.0 / cells)
+    spread_b = over_clips(spread_clip(zb, mean_b), jnp.zeros((1, BOUT), F32))
+    scale_b = lax.rsqrt(spread_b * (1.0 / cells) + EPSILON)
+
+    own = pl.ds(pl.multiple_of(here * 64, 64), 64)
+    hidden_a = act((za[own, :] - mean_a) * scale_a + off_a)
+    hidden_b = act((zb[own, :] - mean_b) * scale_b + off_b)
+    out_ref[...] = jnp.concatenate(
+        [hidden_a[:, :C0], hidden_b, hidden_a[:, IN_OUT:]], axis=1
+    ).astype(BF16)
+
+    def grad_b(c):
+        y = (zb[rows_of(c), :] - mean_b) * scale_b
+        d = cs[rows_of(c), C0 : C0 + BOUT].astype(F32) * slope(y + off_b)
+        return d, y
+
+    def sums_b(c, carry):
+        d, y = grad_b(c)
+        return (
+            carry[0] + jnp.sum(d, axis=0, keepdims=True),
+            carry[1] + jnp.sum(d * y, axis=0, keepdims=True),
+        )
+
+    zero_b = jnp.zeros((1, BOUT), F32)
+    sum_b, cross_b = over_clips(sums_b, (zero_b, zero_b))
+
+    def error_b(c, _):
+        d, y = grad_b(c)
+        e = scale_b * (d - sum_b * (1.0 / cells) - y * (cross_b * (1.0 / cells)))
+        eb[slots_of(c), :] = jnp.where(mask, e, 0.0).astype(BF16)
+        return 0
+
+    over_clips(error_b, 0)
+
+    def picker(rows, cut, part_one, part_two, columns, edge):
+        r = lax.broadcasted_iota(jnp.int32, (rows, columns), 0)
+        k = lax.broadcasted_iota(jnp.int32, (rows, columns), 1)
+        want = jnp.where(r < cut, here * part_one + r, edge + here * part_two + r - cut)
+        return jnp.where(k == want, 1.0, 0.0).astype(BF16)
+
+    pick_b = picker(part_mid + part_small, part_mid, part_mid, part_small, BOUT, C1B)
+    et[...] = dot_nt(pick_b, eb[64 : 64 + wide, :]).astype(BF16)
+    for a in range(3):
+        gm = dot_nn(et[:part_mid, :], um[a * 64 : a * 64 + wide, :])
+        gmid_ref[9 * a : 9 * a + 9] = gm.T.reshape(9, C1A, part_mid)
+        gs = dot_nn(et[part_mid:, :], us[a * 64 : a * 64 + wide, :])
+        gsmall_ref[9 * a : 9 * a + 9] = gs.T.reshape(9, C2A, part_small)
+
+    def grad_a(c, carry):
+        mids, smalls = None, None
+        for a in range(3):
+            one = dot_nt(eb[slots_of(c, 2 - a), :C1B], wmid_ref[a])
+            two = dot_nt(eb[slots_of(c, 2 - a), C1B:], wsmall_ref[a])
+            mids = one if mids is None else mids + one
+            smalls = two if smalls is None else smalls + two
+        back = None
+        for e in range(3):
+            for g in range(3):
+                k = 3 * e + g
+                t = jnp.concatenate(
+                    [mids[:, k * C1A : (k + 1) * C1A], smalls[:, k * C2A : (k + 1) * C2A]], axis=1
+                )
+                t = roll_rows(t, 8 * (e - 1) + g - 1)
+                back = t if back is None else back + t
+        y = normal_a(c, 0, SECTION_A)
+        gain = slope(y + off_a)
+        cot = cs[rows_of(c), :]
+        d = jnp.concatenate([cot[:, :C0].astype(F32), back, cot[:, C0 + BOUT :].astype(F32)], axis=1)
+        d = jnp.where(mask, d * gain, 0.0)
+        da[rows_of(c), :] = d
+        return (
+            carry[0] + jnp.sum(d, axis=0, keepdims=True),
+            carry[1] + jnp.sum(d * y, axis=0, keepdims=True),
+        )
+
+    zero_a = jnp.zeros((1, SECTION_A), F32)
+    sum_a, cross_a = over_clips(grad_a, (zero_a, zero_a))
+    goff_ref[...] = jnp.concatenate([sum_a, sum_b], axis=1)
+
+    def error_a(c, _):
+        y = normal_a(c, 0, SECTION_A)
+        e = scale_a * (da[rows_of(c), :] - sum_a * (1.0 / cells) - y * (cross_a * (1.0 / cells)))
+        e = jnp.where(mask, e, 0.0)
+        ea[slots_of(c), :IN_OUT] = e[:, :IN_OUT].astype(BF16)
+        qs[slots_of(c), :] = e[:, IN_OUT:].astype(BF16).astype(F32)
+        ea[slots_of(c), IN_OUT:] = box(c).astype(BF16)
+        return 0
+
+    over_clips(error_a, 0)
+
+    around = pl.ds(pl.multiple_of(here * 64, 64), 192)
+    dx_ref[...] = dot_nt(ea[around, :IN_OUT], win_ref[...]) + dot_nt(
+        ea[around, IN_OUT:], wpool_ref[...]
+    )
+    pick_a = picker(part_in + part_pool, part_in, part_in, part_pool, SECTION_A, IN_OUT)
+    for c in range(clips):
+        errors = ea[c * slot + 64 : c * slot + 64 + span, :]
+        eat[:, c * span : (c + 1) * span] = dot_nt(pick_a, errors).astype(BF16)
+    gin_ref[...] = dot_nn(eat[:part_in, :], xs[...])
+    gpool_ref[...] = dot_nn(eat[part_in:, :], xs[...])
+
+
+def first_errors(
+    flag_ref, dx_ref, zb_ref, zp_ref, zin_ref, before_ref, after_ref, ma_ref, mb_ref, off_ref,
+    db_ref, yb_ref, dp_ref, yp_ref, dc_ref, st_ref,
+):
+    r = lax.broadcasted_iota(jnp.int32, (256, 64), 0)
+    k = lax.broadcasted_iota(jnp.int32, (256, 64), 1)
+    spread = jnp.where(k == ((r >> 5) << 3) + ((r & 15) >> 1), 1.0, 0.0).astype(BF16)
+
+    def frame_grad(f):
+        d = dx_ref[f * 64 : (f + 1) * 64, :] * 0.125
+        high = d.astype(BF16)
+        low = (d - high.astype(F32)).astype(BF16)
+        return dot_nn(spread, high) + dot_nn(spread, low)
+
+    mean_b, scale_b = mb_ref[0:1, :], mb_ref[1:2, :]
+    off_b, off_p = off_ref[:, SECTION_A:], off_ref[:, IN_OUT:SECTION_A]
+    zero_b, zero_p = jnp.zeros((1, BOUT), F32), jnp.zeros((1, POOL), F32)
+    sums = [zero_b, zero_p, jnp.zeros((1, C0), F32)]
+    crosses = list(sums)
+
+    def add(i, d, y):
+        sums[i] = sums[i] + jnp.sum(d, axis=0, keepdims=True)
+        crosses[i] = crosses[i] + jnp.sum(d * y, axis=0, keepdims=True)
+
+    grads = [frame_grad(f) for f in range(3)]
+    for s in range(4):
+        rows = slice(s * 256, (s + 1) * 256)
+        if s == 0:
+            z_b, z_p = before_ref[:, :BOUT].astype(F32), before_ref[:, BOUT:].astype(F32)
+        elif s == 3:
+            z_b, z_p = after_ref[:, :BOUT].astype(F32), after_ref[:, BOUT:].astype(F32)
+        else:
+            inner = slice((s - 1) * 256, s * 256)
+            z_b, z_p = zb_ref[inner, :], zp_ref[inner, :]
+        g = grads[(s + 1) // 2]
+        y_b = (z_b - mean_b[:, :BOUT]) * scale_b[:, :BOUT]
+        d_b = g[:, C0 : C0 + BOUT] * slope(y_b + off_b)
+        y_p = (z_p - mean_b[:, BOUT:]) * scale_b[:, BOUT:]
+        d_p = g[:, C0 + BOUT :] * slope(y_p + off_p)
+        db_ref[rows, :], yb_ref[rows, :] = d_b, y_b
+        dp_ref[rows, :], yp_ref[rows, :] = d_p, y_p
+        if s in (1, 2):
+            add(0, d_b, y_b)
+            add(1, d_p, y_p)
+            y_c = (zin_ref[inner, :C0] - ma_ref[0:1, :C0]) * ma_ref[1:2, :C0]
+            d_c = g[:, :C0] * slope(y_c + off_ref[:, :C0])
+            dc_ref[inner, :] = d_c
+            add(2, d_c, y_c)
+    store_copies(st_ref, pack_rows(sums + crosses))
+
+
+def first_hidden_back(
+    cells, flag_ref, st_ref, db_ref, yb_ref, zin_ref, ma_ref, mb_ref, off_ref, um_ref, us_ref,
+    wmid_ref, wsmall_ref,
+    dm_ref, st2_ref, sum_ref, gmid_ref, gsmall_ref,
+    eb, etm, ets,
+):
+    here = flag_ref[0]
+    parts = gmid_ref.shape[0]
+    part_mid, part_small = gmid_ref.shape[2], gsmall_ref.shape[2]
+    totals = jnp.sum(st_ref[...], axis=0)
+    sum_ref[...] = totals
+    sum_b, cross_b = unpack_rows(totals, 0, BOUT), unpack_rows(totals, 7, BOUT)
+    scale_b = mb_ref[1:2, :BOUT]
+    frame = valid_first(256)
+    edge = jnp.zeros((16, BOUT), BF16)
+    eb[0:16, :] = edge
+    eb[1040:1056, :] = edge
+    for s in range(4):
+        rows = slice(s * 256, (s + 1) * 256)
+        e = scale_b * (
+            db_ref[rows, :] - sum_b * (1.0 / cells) - yb_ref[rows, :] * (cross_b * (1.0 / cells))
+        )
+        mask = frame
+        if s == 0:
+            mask = frame & (flag_ref[1] > 0)
+        elif s == 3:
+            mask = frame & (flag_ref[2] > 0)
+        eb[16 + s * 256 : 16 + (s + 1) * 256, :] = jnp.where(mask, e, 0.0).astype(BF16)
+
+    sums, crosses = jnp.zeros((1, MID), F32), jnp.zeros((1, MID), F32)
+    for f in range(2):
+        mids, smalls = None, None
+        for a in range(3):
+            for e in range(3):
+                start = 16 + 256 * (f + 1) - (a - 1) * 256 - (e - 1) * 16
+                one = dot_nt(eb[start : start + 256, :C1B], wmid_ref[3 * a + e])
+                two = dot_nt(eb[start : start + 256, C1B:], wsmall_ref[3 * a + e])
+                mids = one if mids is None else mids + one
+                smalls = two if smalls is None else smalls + two
+        back = None
+        for g in range(3):
+            t = jnp.concatenate(
+                [mids[:, g * C1A : (g + 1) * C1A], smalls[:, g * C2A : (g + 1) * C2A]], axis=1
+            )
+            t = roll_rows(t, g - 1)
+            back = t if back is None else back + t
+        rows = slice(f * 256, (f + 1) * 256)
+        y = (zin_ref[rows, C0:] - ma_ref[0:1, C0:]) * ma_ref[1:2, C0:]
+        d = jnp.where(frame, back * slope(y + off_ref[:, C0:IN_OUT]), 0.0)
+        dm_ref[rows, :] = d
+        sums = sums + jnp.sum(d, axis=0, keepdims=True)
+        crosses = crosses + jnp.sum(d * y, axis=0, keepdims=True)
+    store_copies(st2_ref, pack_rows([sums, crosses]))
+
+    def eye(n):
+        r = lax.broadcasted_iota(jnp.int32, (n, n), 0)
+        k = lax.broadcasted_iota(jnp.int32, (n, n), 1)
+        return jnp.where(r == k, 1.0, 0.0).astype(BF16)
+
+    etm[...] = dot_nt(eye(C1B), eb[272:784, :C1B]).astype(BF16)
+    ets[...] = dot_nt(eye(C2B), eb[272:784, C1B:]).astype(BF16)
+    for a in range(3):
+        for e in range(3):
+            start = 16 + a * 256 + (e - 1) * 16
+            gm = dot_nn(etm[...], um_ref[start : start + 512, :]).astype(BF16)
+            gs = dot_nn(ets[...], us_ref[start : start + 512, :]).astype(BF16)
+            for p in range(parts):
+                to = lax.rem(p - here + parts, parts)
+                gmid_ref[to, 3 * a + e] = gm[p * part_mid : (p + 1) * part_mid]
+                gsmall_ref[to, 3 * a + e] = gs[p * part_small : (p + 1) * part_small]
+
+
+def first_input_back(
+    cells, flag_ref, st_ref, sum_ref, dm_ref, dc_ref, dp_ref, yp_ref, zin_ref, ma_ref, mb_ref,
+    x_ref, win_ref, wpool_ref,
+    dx_ref, g_ref, goff_ref,
+    ea,
+):
+    here = flag_ref[0]
+    parts = g_ref.shape[0]
+    part_in, part_pool = IN_OUT // parts, POOL // parts
+    totals = jnp.sum(st_ref[...], axis=0)
+    before = sum_ref[...]
+    sum_m, cross_m = unpack_rows(totals, 0, MID), unpack_rows(totals, 2, MID)
+    sum_b = unpack_rows(before, 0, BOUT)
+    sum_p, sum_c = unpack_rows(before, 4, POOL), unpack_rows(before, 5, C0)
+    cross_p, cross_c = unpack_rows(before, 11, POOL), unpack_rows(before, 12, C0)
+    goff_ref[...] = jnp.concatenate([sum_c, sum_m, sum_p, sum_b], axis=1)
+    share = 1.0 / cells
+    frame = valid_first(256)
+    pools = []
+    for s in range(4):
+        rows = slice(s * 256, (s + 1) * 256)
+        e = mb_ref[1:2, BOUT:] * (
+            dp_ref[rows, :] - sum_p * share - yp_ref[rows, :] * (cross_p * share)
+        )
+        mask = frame
+        if s == 0:
+            mask = frame & (flag_ref[1] > 0)
+        elif s == 3:
+            mask = frame & (flag_ref[2] > 0)
+        pools.append(jnp.where(mask, e, 0.0).astype(BF16).astype(F32))
+    for f in range(2):
+        rows = slice(f * 256, (f + 1) * 256)
+        value = box_plane(pools[f] + pools[f + 1] + pools[f + 2], 16) * (1.0 / 27.0)
+        ea[rows, IN_OUT:] = jnp.where(frame, value, 0.0).astype(BF16)
+        y = (zin_ref[rows, :] - ma_ref[0:1, :]) * ma_ref[1:2, :]
+        e = ma_ref[1:2, :C0] * (dc_ref[rows, :] - sum_c * share - y[:, :C0] * (cross_c * share))
+        ea[rows, :C0] = jnp.where(frame, e, 0.0).astype(BF16)
+        e = ma_ref[1:2, C0:] * (dm_ref[rows, :] - sum_m * share - y[:, C0:] * (cross_m * share))
+        ea[rows, C0:IN_OUT] = jnp.where(frame, e, 0.0).astype(BF16)
+        dx_ref[rows, :] = dot_nt(ea[rows, :IN_OUT], win_ref[...]) + dot_nt(
+            ea[rows, IN_OUT:], wpool_ref[...]
+        )
+    r = lax.broadcasted_iota(jnp.int32, (SECTION_A, SECTION_A), 0)
+    k = lax.broadcasted_iota(jnp.int32, (SECTION_A, SECTION_A), 1)
+    eye = jnp.where(r == k, 1.0, 0.0).astype(BF16)
+    turned = dot_nt(eye, ea[...]).astype(BF16)
+    g = dot_nn(turned, x_ref[...]).astype(BF16)
+    for p in range(parts):
+        to = lax.rem(p - here + parts, parts)
+        g_ref[to, :part_in] = g[p * part_in : (p + 1) * part_in]
+        g_ref[to, part_in:] = g[IN_OUT + p * part_pool : IN_OUT + (p + 1) * part_pool]
+
+
+def call(body, outs, scratch, *args, scalars=1):
+    in_specs = [pl.BlockSpec(memory_space=pltpu.SMEM)] * scalars
+    in_specs += [pl.BlockSpec(memory_space=pltpu.VMEM)] * (len(args) - scalars)
+    return pl.pallas_call(
+        body,
+        out_shape=[jax.ShapeDtypeStruct(s, d) for s, d in outs],
+        in_specs=in_specs,
+        out_specs=[pl.BlockSpec(memory_space=pltpu.VMEM)] * len(outs),
+        scratch_shapes=[pltpu.VMEM(s, d) for s, d in scratch],
+        compiler_params=pltpu.CompilerParams(vmem_limit_bytes=VMEM_LIMIT),
+    )(*args)
+
+
+def exchange(copies):
+    return lax.all_to_all(copies, ("clip", "tm"), 0, 0)
+
+
+def neighbours(head, tail):
+    size = lax.axis_size("tm")
+    up = [(i, i + 1) for i in range(size - 1)]
+    down = [(i + 1, i) for i in range(size - 1)]
+    return lax.ppermute(tail, "tm", up), lax.ppermute(head, "tm", down)
+
+
+def gather_from(value, axis):
+    size = lax.axis_size(axis)
+    blocks = [value]
+    for m in range(1, size):
+        blocks.append(lax.ppermute(value, axis, [((i + m) % size, i) for i in range(size)]))
+    return jnp.stack(blocks)
+
+
+def gather_stream(value):
+    by_clip = gather_from(value, "clip")
+    both = gather_from(by_clip, "tm")
+    return jnp.swapaxes(both, 0, 1).reshape((-1,) + value.shape)
+
+
+def scatter_sum(chunks):
+    size = lax.axis_size("tm")
+    total = chunks[0].astype(F32)
+    for m in range(1, size):
+        sent = lax.ppermute(chunks[m], "tm", [(i, (i + m) % size) for i in range(size)])
+        total = total + sent.astype(F32)
+    return lax.psum(total.astype(BF16), "clip").astype(F32)
+
+
+def small_group(
+    features, w_in_4f, w_pool_4f, w_mid_4f, w_small_4f, offsets_4f,
+    w_in_5b, w_pool_5b, w_mid_5b, w_small_5b, offsets_5b, cotangent,
+):
+    clips, frames = lax.axis_size("clip"), lax.axis_size("tm")
+    group = clips * frames
+    cells = 392.0 * group
+    here = lax.axis_index("tm")
+    flags = jnp.stack([here, here > 0, here < frames - 1]).astype(jnp.int32)
+    offsets_4f, offsets_5b = offsets_4f[None], offsets_5b[None]
+    x = jnp.pad(features[0], ((0, 0), (0, 2), (0, 2), (0, 0))).reshape(512, features.shape[-1])
+    cot = jnp.pad(cotangent[0, 0], ((0, 1), (0, 1), (0, 0))).reshape(64, OUTC)
+    mid_4f, small_4f = w_mid_4f.reshape(9, 3 * C1A, C1B), w_small_4f.reshape(9, 3 * C2A, C2B)
+    mid_5b, small_5b = w_mid_5b.reshape(3, 9 * C1A, C1B), w_small_5b.reshape(3, 9 * C2A, C2B)
+
+    z_in, q, stats, head, tail = call(
+        first_project,
+        [((512, IN_OUT), F32), ((512, POOL), F32), ((group, 8, 128), F32),
+         ((256, MID + POOL), BF16), ((256, MID + POOL), BF16)],
+        [], x, w_in_4f, w_pool_4f, scalars=0,
+    )
+    before, after = neighbours(head, tail)
+    stats = exchange(stats)
+    z_b, z_p, stats, x2_c, u_mid, u_small, head, tail, moments_a = call(
+        first_hidden,
+        [((512, BOUT), F32), ((512, POOL), F32), ((group, 16, 128), F32), ((64, C0), BF16),
+         ((1056, 3 * C1A), BF16), ((1056, 3 * C2A), BF16),
+         ((256, BOUT + POOL), BF16), ((256, BOUT + POOL), BF16), ((2, IN_OUT), F32)],
+        [((1024, MID), F32), ((4, 128, 128), F32)],
+        flags, stats, z_in, q, before, after, mid_4f, small_4f, offsets_4f,
+    )
+    before, after = neighbours(head, tail)
+    x2_c = gather_stream(x2_c)
+    stats = exchange(stats)
+    x2_b, moments_b = call(
+        first_output,
+        [((64, BOUT + POOL), BF16), ((2, BOUT + POOL), F32)],
+        [((4, 128, 128), F32)],
+        stats, z_b, z_p, offsets_4f, scalars=0,
+    )
+    x2_b = gather_stream(x2_b)
+    cot = gather_stream(cot)
+    rows, slots = group * 64, (clips * (frames + 1) + 2) * 64
+    wide = clips * (frames + 1) * 64
+    part = (C1B // frames, C2B // frames, IN_OUT // frames, POOL // frames)
+    out, dx2, g_in_5b, g_pool_5b, g_mid_5b, g_small_5b, g_off_5b = call(
+        functools.partial(second_layer, clips, frames),
+        [((64, OUTC), BF16), ((192, OUTC), F32), ((part[2], OUTC), F32), ((part[3], OUTC), F32),
+         ((27, C1A, part[0]), F32), ((27, C2A, part[1]), F32), ((1, 1024), F32)],
+        [((rows, OUTC), BF16), ((rows, OUTC), BF16), ((rows, SECTION_A), F32), ((rows, BOUT), F32),
+         ((slots, 9 * C1A), BF16), ((slots, 9 * C2A), BF16), ((slots, POOL), F32),
+         ((slots, BOUT), BF16), ((slots, SECTION_A), BF16), ((part[0] + part[1], wide), BF16),
+         ((part[2] + part[3], rows), BF16), ((rows, SECTION_A), F32)],
+        flags, x2_c, x2_b, cot, w_in_5b, w_pool_5b, mid_5b, small_5b, offsets_5b,
+    )
+    d_b, y_b, d_p, y_p, d_c, stats = call(
+        first_errors,
+        [((1024, BOUT), F32), ((1024, BOUT), F32), ((1024, POOL), F32), ((1024, POOL), F32),
+         ((512, C0), F32), ((group, 16, 128), F32)],
+        [], flags, dx2, z_b, z_p, z_in, before, after, moments_a, moments_b, offsets_4f,
+    )
+    stats = exchange(stats)
+    d_m, stats, sums, g_mid, g_small = call(
+        functools.partial(first_hidden_back, cells),
+        [((512, MID), F32), ((group, 8, 128), F32), ((16, 128), F32),
+         ((frames, 9, part[0], 3 * C1A), BF16), ((frames, 9, part[1], 3 * C2A), BF16)],
+        [((1056, BOUT), BF16), ((C1B, 512), BF16), ((C2B, 512), BF16)],
+        flags, stats, d_b, y_b, z_in, moments_a, moments_b, offsets_4f, u_mid, u_small,
+        mid_4f, small_4f,
+    )
+    g_mid, g_small = scatter_sum(g_mid), scatter_sum(g_small)
+    stats = exchange(stats)
+    d_x, g_a, g_off = call(
+        functools.partial(first_input_back, cells),
+        [((512, features.shape[-1]), F32), ((frames, part[2] + part[3], features.shape[-1]), BF16),
+         ((1, 1024), F32)],
+        [((512, SECTION_A), BF16)],
+        flags, stats, sums, d_m, d_c, d_p, y_p, z_in, moments_a, moments_b, x, w_in_4f, w_pool_4f,
+    )
+    g_a = scatter_sum(g_a)
+
+    def offsets_first(g, inner, outer):
+        return jnp.transpose(g.reshape(9, outer, 3, inner), (0, 2, 3, 1)).reshape(27, inner, outer)
+
+    return (
+        out.reshape(1, 1, 8, 8, OUTC)[:, :, :7, :7],
+        d_x.reshape(1, 2, 16, 16, -1)[:, :, :14, :14],
+        g_a[: part[2]].T,
+        g_a[part[2] :].T,
+        offsets_first(g_mid, C1A, part[0]),
+        offsets_first(g_small, C2A, part[1]),
+        g_off[0],
+        g_in_5b.T,
+        g_pool_5b.T,
+        g_mid_5b,
+        g_small_5b,
+        g_off_5b[0],
+    )
+
+
 def solution(mesh):
     placed = (
         P(("stream", "clip"), "tm", None, None, None),
@@ -329,8 +1048,9 @@
         P("stream"),
         P(("stream", "clip"), "tm", None, None, None),
     )
+    group = mesh.shape["clip"] * mesh.shape["tm"]
     return jax.shard_map(
-        shards,
+        small_group if group <= 16 else shards,
         mesh=mesh,
         in_specs=placed,
         out_specs=(

time: 1090 us -> 303 us (0.28); the launches traced: 1080 us -> 302 us
  blocking collectives: 460 us -> 44.8 us
  waiting for transfers between devices: 268 us -> 76.3 us
  local copies, waits for them, and re-layouts: 156 us -> 18.1 us
  Pallas kernels: 0 us -> 71.1 us
  other arithmetic: 83 us -> 13.9 us
  matrix products: 50.6 us -> 0 us
  starting transfers between devices: 41.7 us -> 63.5 us
    psum x12 -> x1, blocking collectives: 460 us -> 30.1 us  [scatter_sum(): return lax.psum(total.astype(BF16), 'clip').astype(F32)]
    unnamed x16 -> x1, waiting for transfers between devices: 102 us -> 0.02 us
    psum x2 -> x1, waiting for transfers between devices: 115 us -> 25.6 us  [scatter_sum(): return lax.psum(total.astype(BF16), 'clip').astype(F32)]
    pallas_call x0 -> x7, Pallas kernels: none -> 71.1 us  [call(): pl.pallas_call(body, out_shape=[jax.ShapeDtypeStruct(s, d) for s, d in ou...]
    unnamed x205 -> x36, local copies, waits for them, and re-layouts: 72.6 us -> 7.94 us
    dot_general x24 -> x0, matrix products: 50.6 us -> none  [the longest x2 16.2 us: block_backward(): jnp.einsum('nfhwk,nfhwo->ko', patch_one, error_one, preferred_element_typ...]
    slice x42 -> x2, local copies, waits for them, and re-layouts: 40.4 us -> 0.72 us  [the longest x1 0.65 us: small_group(): out.reshape(1, 1, 8, 8, OUTC)[:, :, :7, :7]]
    dot_general x6 -> x0, local copies, waits for them, and re-layouts: 22.5 us -> none  [the longest x2 13.5 us: block_backward(): jnp.einsum('nfhwk,nfhwo->ko', patch_one, error_one, preferred_element_typ...]
  transfers between devices with their start and end apart: 26 -> 35, of which waited for: 18 -> 14; matrix products, arithmetic and copies ran while one was open for 16% -> 7% of each run, Pallas kernels for 0% -> 17%
where the time goes in v1:
time: 303 us; the launch traced here: 302 us
  waiting for transfers between devices  76.3 us (25%)
  Pallas kernels  71.1 us (23%)
  starting transfers between devices  63.5 us (21%)
  blocking collectives  44.8 us (15%)
  local copies, waits for them, and re-layouts  18.1 us (6%)
  between operations  14.3 us (5%)
  other arithmetic  13.9 us (5%)
    pallas_call x7, Pallas kernels, call(): pl.pallas_call(body, out_shape=[jax.ShapeDtypeStruct(s, d) for s, d in ou...  71.1 us
    psum x1, blocking collectives, scatter_sum(): return lax.psum(total.astype(BF16), 'clip').astype(F32)  30.1 us
    ppermute x18, waiting for transfers between devices, gather_from(): lax.ppermute(value, axis, [((i + m) % size, i) for i in range(size)])  27.6 us
    psum x1, waiting for transfers between devices, scatter_sum(): return lax.psum(total.astype(BF16), 'clip').astype(F32)  25.6 us
    ppermute x18, starting transfers between devices, gather_from(): lax.ppermute(value, axis, [((i + m) % size, i) for i in range(size)])  23.8 us
    ppermute x9, waiting for transfers between devices, scatter_sum(): lax.ppermute(chunks[m], 'tm', [(i, (i + m) % size) for i in range(size)])  20.2 us
    all_to_all x3, starting transfers between devices, exchange(): return lax.all_to_all(copies, ('clip', 'tm'), 0, 0)  15.6 us
    all_to_all x1, blocking collectives, exchange(): return lax.all_to_all(copies, ('clip', 'tm'), 0, 0)  14.7 us
  transfers between devices with their start and end apart: 35, of which 14 were waited for; matrix products, arithmetic and copies ran while one was open for 7% of the time, Pallas kernels for 17%

profile of v1, /device:TPU:0, one launch (start us, length us, event | category | flops | bytes accessed | tf_op | source)
XLA Modules:
  0.0 302.1 jit_solution(13070235331812065845)
XLA Ops:
  9.3 3.1 %shard_map.211 = (f32[512,448]{1,0:T(8,128)}, f32[512,128]{1,0:T(8,128)}, f32[16,8,128]{2,1,0:T(8,128)}, bf16[256,320]{1,0:T(8,128)(2,1)}, bf16[256,320]{1,0:T(8,128)(2,1)}) custom-call(bf16[512,528]{1,0:T(8,128)(2,1)} %bitcast.104, bf16[528,448]{1,0:T(8,128)(2,1)} %win_ref.4, bf16[528,128]{1,0:T(8,128)(2,1)} %wpool_ref.5), custom_call_target="tpu_custom_call" | custom-call | tf_op jit(solution)/shard_map/pallas_call | solution.py:892
  12.4 8.3 %all-to-all-start = ((f32[16,8,128]{2,1,0:T(8,128)}), f32[16,8,128]{2,1,0:T(8,128)S(1)}, u32[]{:S(2)}, u32[]{:S(2)}) async-start(f32[16,8,128]{2,1,0:T(8,128)} %get-tuple-element.49), calls=%async_computation | async-start | bytes 131072 | tf_op jit(solution)/shard_map/all_to_all | solution.py:903
  20.7 3.8 %collective-permute-start = (bf16[256,320]{1,0:T(8,128)(2,1)}, bf16[256,320]{1,0:T(8,128)(2,1)S(1)}, u32[]{:S(2)}, u32[]{:S(2)}) collective-permute-start(bf16[256,320]{1,0:T(8,128)(2,1)} %get-tuple-element.52), channel_id=1, source_target_pairs={{0,1},{1,2},{2,3},{4,5},{5,6},{6,7},{8,9},{9,10},{10,11},{12,13},{... | collective-permute-start | bytes 491528 | tf_op jit(solution)/shard_map/ppermute | solution.py:910
  31.9 2.8 collective-permute-done.1.after_ref
  35.3 7.7 %shard_map.212 = (f32[512,448]{1,0:T(8,128)}, f32[512,128]{1,0:T(8,128)}, f32[16,16,128]{2,1,0:T(8,128)}, bf16[64,256]{1,0:T(8,128)(2,1)}, bf16[1056,480]{1,0:T(...) custom-call(s32[3]{0:T(128)} %pad_add_fusion.flag_ref, ...), custom_call_target="tpu_custom_call" | custom-call | tf_op jit(solution)/shard_map/pallas_call | solution.py:892
  46.7 3.7 %all-to-all-start.1 = ((f32[16,16,128]{2,1,0:T(8,128)}), f32[16,16,128]{2,1,0:T(8,128)S(1)}, u32[]{:S(2)}, u32[]{:S(2)}) async-start(f32[16,16,128]{2,1,0:T(8,128)} %get-tuple-element.55), calls=%async_computation.1 | async-start | bytes 262144 | tf_op jit(solution)/shard_map/all_to_all | solution.py:903
  50.5 3.8 %collective-permute-start.2 = (bf16[64,256]{1,0:T(8,128)(2,1)}, bf16[64,256]{1,0:T(8,128)(2,1)S(1)}, u32[]{:S(2)}, u32[]{:S(2)}) collective-permute-start(bf16[64,256]{1,0:T(8,128)(2,1)} %get-tuple-element.54), channel_id=1, source_target_pairs={{4,0},{8,4},{12,8},{0,12},{5,1},{9,5},{13,9},{1,13},{6,2},{10,6},{... | collective-permute-start | bytes 98312 | tf_op jit(solution)/shard_map/ppermute | solution.py:917
  61.0 2.4 shard_map.213
  64.2 13.9 %collective-permute-done.6 = bf16[4,64,256]{2,1,0:T(8,128)(2,1)} collective-permute-done((bf16[4,64,256]{2,1,0:T(8,128)(2,1)}, bf16[4,64,256]{2,1,0:T(8,128)(2,1)}, u32[]{:S(2)}, u32[]{:S(2)}) %collective-permute-start.6) | collective-permute-done | bytes 131104 | tf_op jit(solution)/shard_map/ppermute | solution.py:917
  78.1 5.5 %collective-permute-done.9 = bf16[64,576]{1,0:T(8,128)(2,1)S(1)} collective-permute-done((bf16[64,576]{1,0:T(8,128)(2,1)}, bf16[64,576]{1,0:T(8,128)(2,1)S(1)}, u32[]{:S(2)}, u32[]{:S(2)}) %collective-permute-start.9) | collective-permute-done | bytes 73760 | tf_op jit(solution)/shard_map/ppermute | solution.py:917
  90.1 3.1 %collective-permute-done.7 = bf16[4,64,256]{2,1,0:T(8,128)(2,1)} collective-permute-done((bf16[4,64,256]{2,1,0:T(8,128)(2,1)}, bf16[4,64,256]{2,1,0:T(8,128)(2,1)}, u32[]{:S(2)}, u32[]{:S(2)}) %collective-permute-start.7) | collective-permute-done | bytes 131104 | tf_op jit(solution)/shard_map/ppermute | solution.py:917
  98.7 3.9 %collective-permute-start.20 = (bf16[256,576]{1,0:T(8,128)(2,1)S(1)}, bf16[256,576]{1,0:T(8,128)(2,1)S(1)}, u32[]{:S(2)}, u32[]{:S(2)}) collective-permute-start(bf16[256,576]{1,0:T(8,128)(2,1)S(1)} %copy-done.15), channel_id=1, source_target_pairs={{0,1},{1,2},{2,3},{4,5},{5,6},{6,7},{8,9},{9,10},{10,11},{12,13},{... | collective-permute-start | bytes 884744 | tf_op jit(solution)/shard_map/ppermute | solution.py:910
  105.4 3.2 %collective-permute-done.13 = bf16[4,64,576]{2,1,0:T(8,128)(2,1)} collective-permute-done((bf16[4,64,576]{2,1,0:T(8,128)(2,1)}, bf16[4,64,576]{2,1,0:T(8,128)(2,1)}, u32[]{:S(2)}, u32[]{:S(2)}) %collective-permute-start.13) | collective-permute-done | bytes 294944 | tf_op jit(solution)/shard_map/ppermute | solution.py:917
  111.3 34.6 %shard_map.214 = (bf16[64,832]{1,0:T(8,128)(2,1)}, f32[192,832]{1,0:T(8,128)}, f32[112,832]{1,0:T(8,128)}, f32[32,832]{1,0:T(8,128)}, f32[27,160,80]{2,1,0:T(8,1...) custom-call(s32[3]{0:T(128)} %pad_add_fusion.flag_ref, bf16[16,64,256]{2,1,0:T(8,128)(2,1)} %bitcast.109, ...), custom_call_target="tpu_custom_call" | custom-call | tf_op jit(solution)/shard_map/pallas_call | solution.py:892
  146.7 6.2 %shard_map.215 = (f32[1024,448]{1,0:T(8,128)}, f32[1024,448]{1,0:T(8,128)}, f32[1024,128]{1,0:T(8,128)}, f32[1024,128]{1,0:T(8,128)}, f32[512,256]{1,0:T(8,128)}, /*index=5*/f32[16,16,128]{2,1,0:T(8,128)}) custom-call(s32[3]{0:T(128)} %pad_add_fusion.flag_ref, f32[192,832]{1,0:T(8,128)} %get-tuple-element.60.dx_ref, f32[512,448]{1,0:T(8,128)} %get-tuple-element.56.zb_ref, ...), custom_call_target="tpu_custom_call" | custom-call | tf_op jit(solution)/shard_map/pallas_call | solution.py:892
  152.9 14.7 %all_to_all.20.st_ref = f32[16,16,128]{2,1,0:T(8,128)} all-to-all(f32[16,16,128]{2,1,0:T(8,128)} %get-tuple-element.65), channel_id=1, replica_groups=mesh['stream'=2,'clip'=4,'tm'=4] {'clip','tm'}, dimensions={0} | all-to-all | bytes 262144 | tf_op jit(solution)/shard_map/all_to_all | solution.py:903
  167.7 11.2 %shard_map.216 = (f32[512,192]{1,0:T(8,128)}, f32[16,8,128]{2,1,0:T(8,128)}, f32[16,128]{1,0:T(8,128)}, bf16[4,9,80,480]{3,2,1,0:T(8,128)(2,1)}, bf16[4,9,32,96]{3,2,1,0:T(8,128)(2,1)}) custom-call(s32[3]{0:T(128)} %pad_add_fusion.flag_ref, f32[16,16,128]{2,1,0:T(8,128)} %all_to_all.20.st_ref, f32[1024,448]{1,0:T(8,128)} %get-tuple-element.66.db_ref, ...), custom_call_target="tpu_custom_call" | custom-call | tf_op jit(solution)/shard_map/pallas_call | solution.py:892
  178.8 3.5 %all-to-all-start.3 = ((f32[16,8,128]{2,1,0:T(8,128)}), f32[16,8,128]{2,1,0:T(8,128)S(1)}, u32[]{:S(2)}, u32[]{:S(2)}) async-start(f32[16,8,128]{2,1,0:T(8,128)} %get-tuple-element.70), calls=%async_computation.3 | async-start | bytes 131072 | tf_op jit(solution)/shard_map/all_to_all | solution.py:903
  182.4 2.8 slice_bitcast_fusion.2
  190.6 5.9 %shard_map.217 = (f32[512,528]{1,0:T(8,128)}, bf16[4,144,528]{2,1,0:T(8,128)(2,1)}, f32[1,1024]{1,0:T(1,128)}) custom-call(s32[3]{0:T(128)} %pad_add_fusion.flag_ref, f32[16,8,128]{2,1,0:T(8,128)} %copy-done.8, f32[16,128]{1,0:T(8,128)} %get-tuple-element.71.sum_ref, f32[512,192]{1,0:T(8,128)} %get-tuple-element.72.dm_ref, ...), custom_call_target="tpu_custom_call" | custom-call | tf_op jit(solution)/shard_map/pallas_call | solution.py:892
  200.6 14.1 %collective-permute-done.22 = bf16[144,528]{1,0:T(8,128)(2,1)S(1)} collective-permute-done((bf16[144,528]{1,0:T(8,128)(2,1)S(1)}, bf16[144,528]{1,0:T(8,128)(2,1)S(1)}, u32[]{:S(2)}, u32[]{:S(2)}) %collective-permute-start.22) | collective-permute-done | bytes 152096 | tf_op jit(solution)/shard_map/ppermute | solution.py:931
  216.8 3.5 %collective-permute-done.23 = bf16[144,528]{1,0:T(8,128)(2,1)S(1)} collective-permute-done((bf16[144,528]{1,0:T(8,128)(2,1)S(1)}, bf16[144,528]{1,0:T(8,128)(2,1)S(1)}, u32[]{:S(2)}, u32[]{:S(2)}) %collective-permute-start.23) | collective-permute-done | bytes 152096 | tf_op jit(solution)/shard_map/ppermute | solution.py:931
  232.7 30.1 %psum.23 = bf16[27,32,32]{2,1,0:T(8,128)(2,1)S(1)} all-reduce(bf16[27,32,32]{2,1,0:T(8,128)(2,1)S(1)} %bitcast.114), channel_id=1, replica_groups=mesh['stream'=2,'clip'=4,'tm'=4] {'clip'}, use_global_device_ids=true, to_apply=%region_2.3 | all-reduce | flops 27648 | bytes 110592 | tf_op jit(solution)/shard_map/psum | solution.py:933
  265.5 25.6 %all-reduce.5.cloned.1.call-done = (bf16[144,528]{1,0:T(8,128)(2,1)}, bf16[27,160,80]{2,1,0:T(8,128)(2,1)}) async-done(((bf16[144,528]{1,0:T(8,128)(2,1)}, bf16[27,160,80]{2,1,0:T(8,128)(2,1)}), (bf16[144,528]{1,0:T(8,128)(2,1)}, bf16[27,160,80]{2,1,0:T(8,128)(2,1)})) %all-reduce.5.cloned.1.call-update) | async-done | bytes 843280 | tf_op jit(solution)/shard_map/psum | solution.py:933
  (119 shorter events, 70.3 us)
Async XLA Ops:
  12.4 19.4 %all-to-all-start = ((f32[16,8,128]{2,1,0:T(8,128)}), f32[16,8,128]{2,1,0:T(8,128)S(1)}, u32[]{:S(2)}, u32[]{:S(2)}) async-start(f32[16,8,128]{2,1,0:T(8,128)} %get-tuple-element.49), calls=%async_computation | async-start | bytes 131072 | tf_op jit(solution)/shard_map/all_to_all | solution.py:903
  20.7 11.1 %collective-permute-start = (bf16[256,320]{1,0:T(8,128)(2,1)}, bf16[256,320]{1,0:T(8,128)(2,1)S(1)}, u32[]{:S(2)}, u32[]{:S(2)}) collective-permute-start(bf16[256,320]{1,0:T(8,128)(2,1)} %get-tuple-element.52), channel_id=1, source_target_pairs={{0,1},{1,2},{2,3},{4,5},{5,6},{6,7},{8,9},{9,10},{10,11},{12,13},{... | collective-permute-start | bytes 491528 | tf_op jit(solution)/shard_map/ppermute | solution.py:910
  25.9 24.6 %collective-permute-start.16 = (bf16[64,832]{1,0:T(8,128)(2,1)S(1)}, bf16[64,832]{1,0:T(8,128)(2,1)S(1)}, u32[]{:S(2)}, u32[]{:S(2)}) collective-permute-start(bf16[64,832]{1,0:T(8,128)(2,1)S(1)} %get-tuple-element.140), channel_id=1, source_target_pairs={{12,0},{0,4},{4,8},{8,12},{13,1},{1,5},{5,9},{9,13},{14,2},{2,6},{... | collective-permute-start | bytes 319496 | tf_op jit(solution)/shard_map/ppermute | solution.py:917
  27.4 26.8 %collective-permute-start.15 = (bf16[64,832]{1,0:T(8,128)(2,1)S(1)}, bf16[64,832]{1,0:T(8,128)(2,1)S(1)}, u32[]{:S(2)}, u32[]{:S(2)}) collective-permute-start(bf16[64,832]{1,0:T(8,128)(2,1)S(1)} %get-tuple-element.140), channel_id=1, source_target_pairs={{8,0},{12,4},{0,8},{4,12},{9,1},{13,5},{1,9},{5,13},{10,2},{14,6},... | collective-permute-start | bytes 319496 | tf_op jit(solution)/shard_map/ppermute | solution.py:917
  29.8 24.5 %collective-permute-start.14 = (bf16[64,832]{1,0:T(8,128)(2,1)S(1)}, bf16[64,832]{1,0:T(8,128)(2,1)S(1)}, u32[]{:S(2)}, u32[]{:S(2)}) collective-permute-start(bf16[64,832]{1,0:T(8,128)(2,1)S(1)} %get-tuple-element.140), channel_id=1, source_target_pairs={{4,0},{8,4},{12,8},{0,12},{5,1},{9,5},{13,9},{1,13},{6,2},{10,6},{... | collective-permute-start | bytes 319496 | tf_op jit(solution)/shard_map/ppermute | solution.py:917
  43.0 12.9 %collective-permute-start.4 = (bf16[64,256]{1,0:T(8,128)(2,1)}, bf16[64,256]{1,0:T(8,128)(2,1)S(1)}, u32[]{:S(2)}, u32[]{:S(2)}) collective-permute-start(bf16[64,256]{1,0:T(8,128)(2,1)} %get-tuple-element.54), channel_id=1, source_target_pairs={{12,0},{0,4},{4,8},{8,12},{13,1},{1,5},{5,9},{9,13},{14,2},{2,6},{... | collective-permute-start | bytes 98312 | tf_op jit(solution)/shard_map/ppermute | solution.py:917
  44.4 11.5 %collective-permute-start.3 = (bf16[64,256]{1,0:T(8,128)(2,1)}, bf16[64,256]{1,0:T(8,128)(2,1)S(1)}, u32[]{:S(2)}, u32[]{:S(2)}) collective-permute-start(bf16[64,256]{1,0:T(8,128)(2,1)} %get-tuple-element.54), channel_id=1, source_target_pairs={{8,0},{12,4},{0,8},{4,12},{9,1},{13,5},{1,9},{5,13},{10,2},{14,6},... | collective-permute-start | bytes 98312 | tf_op jit(solution)/shard_map/ppermute | solution.py:917
  46.7 13.6 %all-to-all-start.1 = ((f32[16,16,128]{2,1,0:T(8,128)}), f32[16,16,128]{2,1,0:T(8,128)S(1)}, u32[]{:S(2)}, u32[]{:S(2)}) async-start(f32[16,16,128]{2,1,0:T(8,128)} %get-tuple-element.55), calls=%async_computation.1 | async-start | bytes 262144 | tf_op jit(solution)/shard_map/all_to_all | solution.py:903
  54.4 39.9 %collective-permute-start.18 = (bf16[4,64,832]{2,1,0:T(8,128)(2,1)S(1)}, bf16[4,64,832]{2,1,0:T(8,128)(2,1)S(1)}, u32[]{:S(2)}, u32[]{:S(2)}) collective-permute-start(bf16[4,64,832]{2,1,0:T(8,128)(2,1)S(1)} %get-tuple-element.131), channel_id=1, source_target_pairs={{2,0},{3,1},{0,2},{1,3},{6,4},{7,5},{4,6},{5,7},{10,8},{11,9},{8,1... | collective-permute-start | bytes 1277960 | tf_op jit(solution)/shard_map/ppermute | solution.py:917
  56.9 21.2 %collective-permute-start.6 = (bf16[4,64,256]{2,1,0:T(8,128)(2,1)}, bf16[4,64,256]{2,1,0:T(8,128)(2,1)}, u32[]{:S(2)}, u32[]{:S(2)}) collective-permute-start(bf16[4,64,256]{2,1,0:T(8,128)(2,1)} %get-tuple-element.138), channel_id=1, source_target_pairs={{2,0},{3,1},{0,2},{1,3},{6,4},{7,5},{4,6},{5,7},{10,8},{11,9},{8,1... | collective-permute-start | bytes 393224 | tf_op jit(solution)/shard_map/ppermute | solution.py:917
  58.3 40.3 %collective-permute-start.17 = (bf16[4,64,832]{2,1,0:T(8,128)(2,1)S(1)}, bf16[4,64,832]{2,1,0:T(8,128)(2,1)S(1)}, u32[]{:S(2)}, u32[]{:S(2)}) collective-permute-start(bf16[4,64,832]{2,1,0:T(8,128)(2,1)S(1)} %get-tuple-element.131), channel_id=1, source_target_pairs={{1,0},{2,1},{3,2},{0,3},{5,4},{6,5},{7,6},{4,7},{9,8},{10,9},{11,1... | collective-permute-start | bytes 1277960 | tf_op jit(solution)/shard_map/ppermute | solution.py:917
  59.8 42.8 %collective-permute-start.19 = (bf16[4,64,832]{2,1,0:T(8,128)(2,1)S(1)}, bf16[4,64,832]{2,1,0:T(8,128)(2,1)S(1)}, u32[]{:S(2)}, u32[]{:S(2)}) collective-permute-start(bf16[4,64,832]{2,1,0:T(8,128)(2,1)S(1)} %get-tuple-element.131), channel_id=1, source_target_pairs={{3,0},{0,1},{1,2},{2,3},{7,4},{4,5},{5,6},{6,7},{11,8},{8,9},{9,10... | collective-permute-start | bytes 1277960 | tf_op jit(solution)/shard_map/ppermute | solution.py:917
  63.4 14.6 %collective-permute-start.10 = (bf16[64,576]{1,0:T(8,128)(2,1)}, bf16[64,576]{1,0:T(8,128)(2,1)S(1)}, u32[]{:S(2)}, u32[]{:S(2)}) collective-permute-start(bf16[64,576]{1,0:T(8,128)(2,1)} %get-tuple-element.58), channel_id=1, source_target_pairs={{12,0},{0,4},{4,8},{8,12},{13,1},{1,5},{5,9},{9,13},{14,2},{2,6},{... | collective-permute-start | bytes 221192 | tf_op jit(solution)/shard_map/ppermute | solution.py:917
  89.0 16.5 %collective-permute-start.12 = (bf16[4,64,576]{2,1,0:T(8,128)(2,1)}, bf16[4,64,576]{2,1,0:T(8,128)(2,1)}, u32[]{:S(2)}, u32[]{:S(2)}) collective-permute-start(bf16[4,64,576]{2,1,0:T(8,128)(2,1)} %get-tuple-element.133), channel_id=1, source_target_pairs={{2,0},{3,1},{0,2},{1,3},{6,4},{7,5},{4,6},{5,7},{10,8},{11,9},{8,1... | collective-permute-start | bytes 884744 | tf_op jit(solution)/shard_map/ppermute | solution.py:917
  93.2 12.3 %collective-permute-start.11 = (bf16[4,64,576]{2,1,0:T(8,128)(2,1)}, bf16[4,64,576]{2,1,0:T(8,128)(2,1)}, u32[]{:S(2)}, u32[]{:S(2)}) collective-permute-start(bf16[4,64,576]{2,1,0:T(8,128)(2,1)} %get-tuple-element.133), channel_id=1, source_target_pairs={{1,0},{2,1},{3,2},{0,3},{5,4},{6,5},{7,6},{4,7},{9,8},{10,9},{11,1... | collective-permute-start | bytes 884744 | tf_op jit(solution)/shard_map/ppermute | solution.py:917
  94.3 14.3 %collective-permute-start.13 = (bf16[4,64,576]{2,1,0:T(8,128)(2,1)}, bf16[4,64,576]{2,1,0:T(8,128)(2,1)}, u32[]{:S(2)}, u32[]{:S(2)}) collective-permute-start(bf16[4,64,576]{2,1,0:T(8,128)(2,1)} %get-tuple-element.133), channel_id=1, source_target_pairs={{3,0},{0,1},{1,2},{2,3},{7,4},{4,5},{5,6},{6,7},{11,8},{8,9},{9,10... | collective-permute-start | bytes 884744 | tf_op jit(solution)/shard_map/ppermute | solution.py:917
  98.7 47.2 %collective-permute-start.20 = (bf16[256,576]{1,0:T(8,128)(2,1)S(1)}, bf16[256,576]{1,0:T(8,128)(2,1)S(1)}, u32[]{:S(2)}, u32[]{:S(2)}) collective-permute-start(bf16[256,576]{1,0:T(8,128)(2,1)S(1)} %copy-done.15), channel_id=1, source_target_pairs={{0,1},{1,2},{2,3},{4,5},{5,6},{6,7},{8,9},{9,10},{10,11},{12,13},{... | collective-permute-start | bytes 884744 | tf_op jit(solution)/shard_map/ppermute | solution.py:910
  102.6 43.3 %collective-permute-start.21 = (bf16[256,576]{1,0:T(8,128)(2,1)S(1)}, bf16[256,576]{1,0:T(8,128)(2,1)S(1)}, u32[]{:S(2)}, u32[]{:S(2)}) collective-permute-start(bf16[256,576]{1,0:T(8,128)(2,1)S(1)} %copy-done.14), channel_id=1, source_target_pairs={{1,0},{2,1},{3,2},{5,4},{6,5},{7,6},{9,8},{10,9},{11,10},{13,12},{... | collective-permute-start | bytes 884744 | tf_op jit(solution)/shard_map/ppermute | solution.py:910
  182.3 108.8 %all-reduce.5.cloned.1.call-start = ((), (), s32[]{:S(2)}) async-start(), calls=%async_computation.4 | async-start | bytes 2580480 | tf_op jit(solution)/shard_map/psum | solution.py:933
  185.2 36.8 %collective-permute-start.25 = (bf16[9,80,480]{2,1,0:T(8,128)(2,1)}, bf16[9,80,480]{2,1,0:T(8,128)(2,1)S(1)}, u32[]{:S(2)}, u32[]{:S(2)}) collective-permute-start(bf16[9,80,480]{2,1,0:T(8,128)(2,1)} %get-tuple-element.124), channel_id=1, source_target_pairs={{0,1},{1,2},{2,3},{3,0},{4,5},{5,6},{6,7},{7,4},{8,9},{9,10},{10,1... | collective-permute-start | bytes 2073608 | tf_op jit(solution)/shard_map/ppermute | solution.py:931
  187.0 35.0 %collective-permute-start.27 = (bf16[9,80,480]{2,1,0:T(8,128)(2,1)}, bf16[9,80,480]{2,1,0:T(8,128)(2,1)S(1)}, u32[]{:S(2)}, u32[]{:S(2)}) collective-permute-start(bf16[9,80,480]{2,1,0:T(8,128)(2,1)} %get-tuple-element.125), channel_id=1, source_target_pairs={{0,3},{1,0},{2,1},{3,2},{4,7},{5,4},{6,5},{7,6},{8,11},{9,8},{10,9... | collective-permute-start | bytes 2073608 | tf_op jit(solution)/shard_map/ppermute | solution.py:931
  188.1 33.9 %collective-permute-start.26 = (bf16[9,80,480]{2,1,0:T(8,128)(2,1)S(1)}, bf16[9,80,480]{2,1,0:T(8,128)(2,1)S(1)}, u32[]{:S(2)}, u32[]{:S(2)}) collective-permute-start(bf16[9,80,480]{2,1,0:T(8,128)(2,1)S(1)} %get-tuple-element.126), channel_id=1, source_target_pairs={{0,2},{1,3},{2,0},{3,1},{4,6},{5,7},{6,4},{7,5},{8,10},{9,11},{10,... | collective-permute-start | bytes 2073608 | tf_op jit(solution)/shard_map/ppermute | solution.py:931
  197.6 17.1 %collective-permute-start.22 = (bf16[144,528]{1,0:T(8,128)(2,1)S(1)}, bf16[144,528]{1,0:T(8,128)(2,1)S(1)}, u32[]{:S(2)}, u32[]{:S(2)}) collective-permute-start(bf16[144,528]{1,0:T(8,128)(2,1)S(1)} %get-tuple-element.127), channel_id=1, source_target_pairs={{0,1},{1,2},{2,3},{3,0},{4,5},{5,6},{6,7},{7,4},{8,9},{9,10},{10,1... | collective-permute-start | bytes 456200 | tf_op jit(solution)/shard_map/ppermute | solution.py:931
  199.8 17.0 %collective-permute-start.24 = (bf16[144,528]{1,0:T(8,128)(2,1)S(1)}, bf16[144,528]{1,0:T(8,128)(2,1)S(1)}, u32[]{:S(2)}, u32[]{:S(2)}) collective-permute-start(bf16[144,528]{1,0:T(8,128)(2,1)S(1)} %get-tuple-element.128), channel_id=1, source_target_pairs={{0,3},{1,0},{2,1},{3,2},{4,7},{5,4},{6,5},{7,6},{8,11},{9,8},{10,9... | collective-permute-start | bytes 456200 | tf_op jit(solution)/shard_map/ppermute | solution.py:931
  (27 other events, 211.0 us)
Sparse Core Ops, SparseCore 0:
  225.1 65.9 all-reduce.4

commit v2 on v1

--- a/solution.py
+++ b/solution.py
@@ -324,7 +324,7 @@
 BOUT = 448
 POOL = 128
 OUTC = 832
-VMEM_LIMIT = 56 * 1024 * 1024
+VMEM_LIMIT = 60 * 1024 * 1024
 
 
 def dot_nn(a, b):
@@ -339,6 +339,12 @@
     rows = value.shape[0]
     shift %= rows
     return value if shift == 0 else pltpu.roll(value, shift, 0)
+
+
+def eye(n):
+    r = lax.broadcasted_iota(jnp.int32, (n, n), 0)
+    k = lax.broadcasted_iota(jnp.int32, (n, n), 1)
+    return jnp.where(r == k, 1.0, 0.0).astype(BF16)
 
 
 def valid_first(rows):
@@ -421,7 +427,7 @@
     return value + roll_rows(value, 1) + roll_rows(value, -1)
 
 
-def first_project(x_ref, win_ref, wpool_ref, zin_ref, q_ref, st_ref, head_ref, tail_ref):
+def first_project(x_ref, win_ref, wpool_ref, zin_ref, q_ref, st_ref):
     for f in range(2):
         rows = pl.ds(f * 256, 256)
         x = x_ref[rows, :]
@@ -429,16 +435,13 @@
         q_ref[rows, :] = dot_nn(x, wpool_ref[...])
     total, squares = local_moments(zin_ref[...], valid_first(512), 392)
     store_copies(st_ref, pack_rows([total, squares]))
-    for f, ref in ((0, head_ref), (1, tail_ref)):
-        rows = pl.ds(f * 256, 256)
-        ref[:, :MID] = zin_ref[rows, C0:].astype(BF16)
-        ref[:, MID:] = q_ref[rows, :].astype(BF16)
 
 
 def first_hidden(
-    flag_ref, st_ref, zin_ref, q_ref, before_ref, after_ref, wmid_ref, wsmall_ref, off_ref,
-    zb_ref, zp_ref, st2_ref, x2_ref, um_ref, us_ref, head_ref, tail_ref, ma_ref,
-    mid, half,
+    flag_ref, st_ref, zin_ref, q_ref, before_ref, after_ref, win_ref, wpool_ref, wmid_ref,
+    wsmall_ref, off_ref,
+    zb_ref, zp_ref, st2_ref, x2_ref, mt_ref, head_ref, tail_ref, ma_ref,
+    mid, um_ref, us_ref, half,
 ):
     mean_rows, scale_rows = joint_moments(st_ref[...], 4, 392.0)
     mean, scale = unpack_rows(mean_rows, 0, IN_OUT), unpack_rows(scale_rows, 0, IN_OUT)
@@ -450,10 +453,12 @@
     def middle(z, mask):
         return jnp.where(mask, act((z - mean[:, C0:]) * scale[:, C0:] + off[:, C0:]), 0.0)
 
-    mid[0:256, :] = middle(before_ref[:, :MID].astype(F32), frame & prev)
+    blank = jnp.zeros((32, MID), F32)
+    for start, ref, mask in ((0, before_ref, prev), (768, after_ref, after)):
+        z = jnp.concatenate([dot_nn(ref[...], win_ref[:, C0:]), blank], axis=0)
+        mid[start : start + 256, :] = middle(z, frame & mask)
     mid[256:512, :] = middle(zin_ref[0:256, C0:], frame)
     mid[512:768, :] = middle(zin_ref[256:512, C0:], frame)
-    mid[768:1024, :] = middle(after_ref[:, :MID].astype(F32), frame & after)
     for ref in (um_ref, us_ref):
         edge = jnp.zeros((16, ref.shape[1]), BF16)
         ref[0:16, :] = edge
@@ -482,10 +487,9 @@
 
     first, last = q_ref[0:256, :], q_ref[256:512, :]
     pair = first + last
-    for f, value in (
-        (0, pair + before_ref[:, MID:].astype(F32)),
-        (1, pair + after_ref[:, MID:].astype(F32)),
-    ):
+    for f, ref in ((0, before_ref), (1, after_ref)):
+        beside = jnp.concatenate([dot_nn(ref[...], wpool_ref[...]), blank[:, :POOL]], axis=0)
+        value = pair + beside
         value = box_plane(value, 16) * (1.0 / 27.0)
         zp_ref[f * 256 : (f + 1) * 256, :] = jnp.where(frame, value, 0.0)
 
@@ -494,28 +498,38 @@
     total_p, squares_p = local_moments(zp_ref[...], both, 392)
     store_copies(st2_ref, pack_rows([total_b, total_p, squares_b, squares_p]))
     for f, ref in ((0, head_ref), (1, tail_ref)):
-        rows = pl.ds(f * 256, 256)
+        rows = pl.ds(f * 256, 224)
         ref[:, :BOUT] = zb_ref[rows, :].astype(BF16)
         ref[:, BOUT:] = zp_ref[rows, :].astype(BF16)
     hidden = act((zin_ref[:, :C0] - mean[:, :C0]) * scale[:, :C0] + off[:, :C0])
     x2_ref[...] = halve(jnp.where(both, hidden, 0.0), half, BF16)
-
-
-def first_output(st_ref, zb_ref, zp_ref, off_ref, x2_ref, mb_ref, half):
+    mt_ref[...] = dot_nt(eye(MID), mid[256:768, :].astype(BF16)).astype(BF16)
+
+
+def first_output(st_ref, zb_ref, zp_ref, x2c_ref, off_ref, x2_ref, mb_ref, half):
     mean_rows, scale_rows = joint_moments(st_ref[...], 5, 392.0)
     both = valid_first(512)
     moments = []
     for start, width, z_ref, offset in ((0, BOUT, zb_ref, SECTION_A), (4, POOL, zp_ref, IN_OUT)):
         mean, scale = unpack_rows(mean_rows, start, width), unpack_rows(scale_rows, start, width)
         hidden = act((z_ref[...] - mean) * scale + off_ref[:, offset : offset + width])
-        into = slice(0, BOUT) if start == 0 else slice(BOUT, BOUT + POOL)
+        into = slice(C0, C0 + BOUT) if start == 0 else slice(C0 + BOUT, OUTC)
         x2_ref[:, into] = halve(jnp.where(both, hidden, 0.0), half, BF16)
         moments.append(jnp.concatenate([mean, scale], axis=0))
+    x2_ref[:, :C0] = x2c_ref[...]
     mb_ref[...] = jnp.concatenate(moments, axis=1)
 
 
 def second_layer(
-    clips, frames, flag_ref, x0_ref, x1_ref, cot_ref, win_ref, wpool_ref, wmid_ref, wsmall_ref,
+    clips, frames, flag_ref, *refs,
+):
+    x_refs, refs = refs[:frames], refs[frames:]
+    cot_refs, refs = refs[:frames], refs[frames:]
+    second_layer_body(clips, frames, flag_ref, x_refs, cot_refs, *refs)
+
+
+def second_layer_body(
+    clips, frames, flag_ref, x_refs, cot_refs, win_ref, wpool_ref, wmid_ref, wsmall_ref,
     off_ref,
     out_ref, dx_ref, gin_ref, gpool_ref, gmid_ref, gsmall_ref, goff_ref,
     xs, cs, za, zb, um, us, qs, eb, ea, et, eat, da,
@@ -533,9 +547,8 @@
         for m in range(frames):
             frame = lax.rem(here + m, frames)
             rows = pl.ds(pl.multiple_of(c * span + frame * 64, 64), 64)
-            xs[rows, :C0] = x0_ref[c * frames + m]
-            xs[rows, C0:] = x1_ref[c * frames + m]
-            cs[rows, :] = cot_ref[c * frames + m]
+            xs[rows, :] = x_refs[m][c]
+            cs[rows, :] = cot_refs[m][c]
     for ref in (um, us, qs, eb, ea):
         blank = jnp.zeros((64, ref.shape[1]), ref.dtype)
         for c in range(clips + 1):
@@ -730,6 +743,10 @@
     sums = [zero_b, zero_p, jnp.zeros((1, C0), F32)]
     crosses = list(sums)
 
+    def framed(ref, lanes):
+        value = ref[:, lanes].astype(F32)
+        return jnp.concatenate([value, jnp.zeros((32, value.shape[1]), F32)], axis=0)
+
     def add(i, d, y):
         sums[i] = sums[i] + jnp.sum(d, axis=0, keepdims=True)
         crosses[i] = crosses[i] + jnp.sum(d * y, axis=0, keepdims=True)
@@ -738,9 +755,9 @@
     for s in range(4):
         rows = slice(s * 256, (s + 1) * 256)
         if s == 0:
-            z_b, z_p = before_ref[:, :BOUT].astype(F32), before_ref[:, BOUT:].astype(F32)
+            z_b, z_p = framed(before_ref, slice(0, BOUT)), framed(before_ref, slice(BOUT, None))
         elif s == 3:
-            z_b, z_p = after_ref[:, :BOUT].astype(F32), after_ref[:, BOUT:].astype(F32)
+            z_b, z_p = framed(after_ref, slice(0, BOUT)), framed(after_ref, slice(BOUT, None))
         else:
             inner = slice((s - 1) * 256, s * 256)
             z_b, z_p = zb_ref[inner, :], zp_ref[inner, :]
@@ -749,27 +766,26 @@
         d_b = g[:, C0 : C0 + BOUT] * slope(y_b + off_b)
         y_p = (z_p - mean_b[:, BOUT:]) * scale_b[:, BOUT:]
         d_p = g[:, C0 + BOUT :] * slope(y_p + off_p)
-        db_ref[rows, :], yb_ref[rows, :] = d_b, y_b
-        dp_ref[rows, :], yp_ref[rows, :] = d_p, y_p
+        db_ref[rows, :], yb_ref[rows, :] = d_b.astype(BF16), y_b.astype(BF16)
+        dp_ref[rows, :], yp_ref[rows, :] = d_p.astype(BF16), y_p.astype(BF16)
         if s in (1, 2):
             add(0, d_b, y_b)
             add(1, d_p, y_p)
             y_c = (zin_ref[inner, :C0] - ma_ref[0:1, :C0]) * ma_ref[1:2, :C0]
             d_c = g[:, :C0] * slope(y_c + off_ref[:, :C0])
-            dc_ref[inner, :] = d_c
+            dc_ref[inner, :] = d_c.astype(BF16)
             add(2, d_c, y_c)
     store_copies(st_ref, pack_rows(sums + crosses))
 
 
 def first_hidden_back(
-    cells, flag_ref, st_ref, db_ref, yb_ref, zin_ref, ma_ref, mb_ref, off_ref, um_ref, us_ref,
-    wmid_ref, wsmall_ref,
-    dm_ref, st2_ref, sum_ref, gmid_ref, gsmall_ref,
-    eb, etm, ets,
+    cells, flag_ref, st_ref, db_ref, yb_ref, zin_ref, ma_ref, mb_ref, off_ref, wmid_ref, wsmall_ref,
+    dm_ref, st2_ref, sum_ref, ec_ref,
+    eb,
 ):
+    parts = ec_ref.shape[0]
+    part_mid, part_small = C1B // parts, C2B // parts
     here = flag_ref[0]
-    parts = gmid_ref.shape[0]
-    part_mid, part_small = gmid_ref.shape[2], gsmall_ref.shape[2]
     totals = jnp.sum(st_ref[...], axis=0)
     sum_ref[...] = totals
     sum_b, cross_b = unpack_rows(totals, 0, BOUT), unpack_rows(totals, 7, BOUT)
@@ -781,14 +797,23 @@
     for s in range(4):
         rows = slice(s * 256, (s + 1) * 256)
         e = scale_b * (
-            db_ref[rows, :] - sum_b * (1.0 / cells) - yb_ref[rows, :] * (cross_b * (1.0 / cells))
+            db_ref[rows, :].astype(F32)
+            - sum_b * (1.0 / cells)
+            - yb_ref[rows, :].astype(F32) * (cross_b * (1.0 / cells))
         )
         mask = frame
         if s == 0:
             mask = frame & (flag_ref[1] > 0)
         elif s == 3:
             mask = frame & (flag_ref[2] > 0)
-        eb[16 + s * 256 : 16 + (s + 1) * 256, :] = jnp.where(mask, e, 0.0).astype(BF16)
+        e = jnp.where(mask, e, 0.0)
+        eb[16 + s * 256 : 16 + (s + 1) * 256, :] = e.astype(BF16)
+        if s in (1, 2):
+            for p in range(parts):
+                one = e[:224, p * part_mid : (p + 1) * part_mid]
+                two = e[:224, C1B + p * part_small : C1B + (p + 1) * part_small]
+                into = slice((s - 1) * 224, s * 224)
+                ec_ref[lax.rem(p - here + parts, parts), into, :] = jnp.concatenate([one, two], axis=1).astype(BF16)
 
     sums, crosses = jnp.zeros((1, MID), F32), jnp.zeros((1, MID), F32)
     for f in range(2):
@@ -815,32 +840,72 @@
         crosses = crosses + jnp.sum(d * y, axis=0, keepdims=True)
     store_copies(st2_ref, pack_rows([sums, crosses]))
 
-    def eye(n):
-        r = lax.broadcasted_iota(jnp.int32, (n, n), 0)
-        k = lax.broadcasted_iota(jnp.int32, (n, n), 1)
-        return jnp.where(r == k, 1.0, 0.0).astype(BF16)
-
-    etm[...] = dot_nt(eye(C1B), eb[272:784, :C1B]).astype(BF16)
-    ets[...] = dot_nt(eye(C2B), eb[272:784, C1B:]).astype(BF16)
+
+def first_kernel_grad(
+    flag_ref, own_ref, *refs,
+):
+    parts = own_ref.shape[0]
+    errors = [own_ref.at[0]] + list(refs[: parts - 1])
+    hidden = refs[parts - 1 : 2 * parts - 1]
+    part_ref, em, es, turned = refs[2 * parts - 1 :]
+    frames = 2 * parts
+    chunks = part_ref.shape[0]
+    part_mid = em.shape[1] // 9
+    here, clip = flag_ref[0], flag_ref[3]
+    for m in range(parts):
+        source = lax.rem(here - m + parts, parts)
+        turned[:, pl.ds(pl.multiple_of(source * 512, 512), 512)] = hidden[m][...]
+        for f in range(2):
+            e = errors[m][f * 224 : f * 224 + 224, :].astype(F32)
+            e = jnp.concatenate([e, jnp.zeros((32, e.shape[1]), F32)], axis=0)
+            moved = []
+            for i in range(3):
+                row = roll_rows(e, 16 * (i - 1))
+                moved += [roll_rows(row, g - 1) for g in range(3)]
+            rows = pl.ds(pl.multiple_of(source * 512 + f * 256, 256), 256)
+            em[rows, :] = jnp.concatenate([v[:, :part_mid] for v in moved], axis=1).astype(BF16)
+            es[rows, :] = jnp.concatenate([v[:, part_mid:] for v in moved], axis=1).astype(BF16)
+    mids, smalls = [], []
     for a in range(3):
-        for e in range(3):
-            start = 16 + a * 256 + (e - 1) * 16
-            gm = dot_nn(etm[...], um_ref[start : start + 512, :]).astype(BF16)
-            gs = dot_nn(ets[...], us_ref[start : start + 512, :]).astype(BF16)
-            for p in range(parts):
-                to = lax.rem(p - here + parts, parts)
-                gmid_ref[to, 3 * a + e] = gm[p * part_mid : (p + 1) * part_mid]
-                gsmall_ref[to, 3 * a + e] = gs[p * part_small : (p + 1) * part_small]
+        shift = 256 * (a - 1)
+        lo, hi = max(0, shift), min(frames * 256, frames * 256 + shift)
+        lanes, rows = slice(lo, hi), slice(lo - shift, hi - shift)
+        mids.append(dot_nn(turned[:C1A, lanes], em[rows, :]))
+        smalls.append(dot_nn(turned[C1A:, lanes], es[rows, :]))
+    mids, smalls = jnp.concatenate(mids, axis=1), jnp.concatenate(smalls, axis=1)
+    high, low = C1A // chunks, C2A // chunks
+    wide = smalls.shape[1] // chunks
+    for i in range(chunks):
+        tail = [smalls[i * low : (i + 1) * low, q * wide : (q + 1) * wide] for q in range(chunks)]
+        tail = jnp.concatenate(tail + [jnp.zeros((high - C2A, wide), F32)], axis=0)
+        value = jnp.concatenate([mids[i * high : (i + 1) * high], tail], axis=1).astype(BF16)
+        part_ref[lax.rem(i - clip + chunks, chunks)] = value
+
+
+def first_kernel_join(flag_ref, *refs):
+    chunks = len(refs) - 2
+    gmid_ref, gsmall_ref = refs[chunks:]
+    high, low = C1A // chunks, C2A // chunks
+    part_mid, part_small = gmid_ref.shape[2], gsmall_ref.shape[2]
+    for m in range(chunks):
+        at = lax.rem(flag_ref[3] + m, chunks)
+        value = refs[m][...].astype(F32)
+        rows = pl.ds(pl.multiple_of(at * high, 8), high)
+        for k in range(27):
+            gmid_ref[k, rows, :] = value[:, k * part_mid : (k + 1) * part_mid]
+        small = [value[q * low : (q + 1) * low, 27 * part_mid :] for q in range(chunks)]
+        small = jnp.concatenate(small, axis=1)
+        rows = pl.ds(pl.multiple_of(at * low, 8), low)
+        for k in range(27):
+            gsmall_ref[k, rows, :] = small[:, k * part_small : (k + 1) * part_small]
 
 
 def first_input_back(
-    cells, flag_ref, st_ref, sum_ref, dm_ref, dc_ref, dp_ref, yp_ref, zin_ref, ma_ref, mb_ref,
+    cells, parts, flag_ref, st_ref, sum_ref, dm_ref, dc_ref, dp_ref, yp_ref, zin_ref, ma_ref, mb_ref,
     x_ref, win_ref, wpool_ref,
     dx_ref, g_ref, goff_ref,
     ea,
 ):
-    here = flag_ref[0]
-    parts = g_ref.shape[0]
     part_in, part_pool = IN_OUT // parts, POOL // parts
     totals = jnp.sum(st_ref[...], axis=0)
     before = sum_ref[...]
@@ -855,7 +920,9 @@
     for s in range(4):
         rows = slice(s * 256, (s + 1) * 256)
         e = mb_ref[1:2, BOUT:] * (
-            dp_ref[rows, :] - sum_p * share - yp_ref[rows, :] * (cross_p * share)
+            dp_ref[rows, :].astype(F32)
+            - sum_p * share
+            - yp_ref[rows, :].astype(F32) * (cross_p * share)
         )
         mask = frame
         if s == 0:
@@ -868,25 +935,22 @@
         value = box_plane(pools[f] + pools[f + 1] + pools[f + 2], 16) * (1.0 / 27.0)
         ea[rows, IN_OUT:] = jnp.where(frame, value, 0.0).astype(BF16)
         y = (zin_ref[rows, :] - ma_ref[0:1, :]) * ma_ref[1:2, :]
-        e = ma_ref[1:2, :C0] * (dc_ref[rows, :] - sum_c * share - y[:, :C0] * (cross_c * share))
+        e = dc_ref[rows, :].astype(F32) - sum_c * share - y[:, :C0] * (cross_c * share)
+        e = ma_ref[1:2, :C0] * e
         ea[rows, :C0] = jnp.where(frame, e, 0.0).astype(BF16)
         e = ma_ref[1:2, C0:] * (dm_ref[rows, :] - sum_m * share - y[:, C0:] * (cross_m * share))
         ea[rows, C0:IN_OUT] = jnp.where(frame, e, 0.0).astype(BF16)
         dx_ref[rows, :] = dot_nt(ea[rows, :IN_OUT], win_ref[...]) + dot_nt(
             ea[rows, IN_OUT:], wpool_ref[...]
         )
-    r = lax.broadcasted_iota(jnp.int32, (SECTION_A, SECTION_A), 0)
-    k = lax.broadcasted_iota(jnp.int32, (SECTION_A, SECTION_A), 1)
-    eye = jnp.where(r == k, 1.0, 0.0).astype(BF16)
-    turned = dot_nt(eye, ea[...]).astype(BF16)
+    turned = dot_nt(eye(SECTION_A), ea[...]).astype(BF16)
     g = dot_nn(turned, x_ref[...]).astype(BF16)
     for p in range(parts):
-        to = lax.rem(p - here + parts, parts)
-        g_ref[to, :part_in] = g[p * part_in : (p + 1) * part_in]
-        g_ref[to, part_in:] = g[IN_OUT + p * part_pool : IN_OUT + (p + 1) * part_pool]
-
-
-def call(body, outs, scratch, *args, scalars=1):
+        g_ref[p, :part_in] = g[p * part_in : (p + 1) * part_in]
+        g_ref[p, part_in:] = g[IN_OUT + p * part_pool : IN_OUT + (p + 1) * part_pool]
+
+
+def call(body, outs, scratch, *args, scalars=1, limit=VMEM_LIMIT, us=1):
     in_specs = [pl.BlockSpec(memory_space=pltpu.SMEM)] * scalars
     in_specs += [pl.BlockSpec(memory_space=pltpu.VMEM)] * (len(args) - scalars)
     return pl.pallas_call(
@@ -895,7 +959,12 @@
         in_specs=in_specs,
         out_specs=[pl.BlockSpec(memory_space=pltpu.VMEM)] * len(outs),
         scratch_shapes=[pltpu.VMEM(s, d) for s, d in scratch],
-        compiler_params=pltpu.CompilerParams(vmem_limit_bytes=VMEM_LIMIT),
+        compiler_params=pltpu.CompilerParams(vmem_limit_bytes=limit),
+        cost_estimate=pl.CostEstimate(
+            flops=int(us * 1.1e9),
+            bytes_accessed=sum(a.size * a.dtype.itemsize for a in args),
+            transcendentals=0,
+        ),
     )(*args)
 
 
@@ -910,27 +979,37 @@
     return lax.ppermute(tail, "tm", up), lax.ppermute(head, "tm", down)
 
 
-def gather_from(value, axis):
+def gather_from(value, axis, back=False):
     size = lax.axis_size(axis)
     blocks = [value]
     for m in range(1, size):
-        blocks.append(lax.ppermute(value, axis, [((i + m) % size, i) for i in range(size)]))
-    return jnp.stack(blocks)
-
-
-def gather_stream(value):
-    by_clip = gather_from(value, "clip")
-    both = gather_from(by_clip, "tm")
-    return jnp.swapaxes(both, 0, 1).reshape((-1,) + value.shape)
-
-
-def scatter_sum(chunks):
-    size = lax.axis_size("tm")
-    total = chunks[0].astype(F32)
+        step = -m if back else m
+        blocks.append(lax.ppermute(value, axis, [((i + step) % size, i) for i in range(size)]))
+    return blocks
+
+
+def hand_on(chunks, axis):
+    size = lax.axis_size(axis)
+    blocks = [chunks[0]]
     for m in range(1, size):
-        sent = lax.ppermute(chunks[m], "tm", [(i, (i + m) % size) for i in range(size)])
-        total = total + sent.astype(F32)
-    return lax.psum(total.astype(BF16), "clip").astype(F32)
+        blocks.append(lax.ppermute(chunks[m], axis, [(i, (i + m) % size) for i in range(size)]))
+    return blocks
+
+
+def to_all(value, axis):
+    size = lax.axis_size(axis)
+    return lax.all_to_all(jnp.broadcast_to(value[None], (size,) + value.shape), axis, 0, 0)
+
+
+def summed(parts):
+    total = parts[0].astype(F32)
+    for i in range(1, len(parts)):
+        total = total + parts[i].astype(F32)
+    return total.astype(BF16)
+
+
+def after(value, *others):
+    return lax.optimization_barrier((value,) + others)[0]
 
 
 def small_group(
@@ -941,40 +1020,44 @@
     group = clips * frames
     cells = 392.0 * group
     here = lax.axis_index("tm")
-    flags = jnp.stack([here, here > 0, here < frames - 1]).astype(jnp.int32)
+    flags = jnp.stack([here, here > 0, here < frames - 1, lax.axis_index("clip")]).astype(jnp.int32)
     offsets_4f, offsets_5b = offsets_4f[None], offsets_5b[None]
     x = jnp.pad(features[0], ((0, 0), (0, 2), (0, 2), (0, 0))).reshape(512, features.shape[-1])
     cot = jnp.pad(cotangent[0, 0], ((0, 1), (0, 1), (0, 0))).reshape(64, OUTC)
     mid_4f, small_4f = w_mid_4f.reshape(9, 3 * C1A, C1B), w_small_4f.reshape(9, 3 * C2A, C2B)
     mid_5b, small_5b = w_mid_5b.reshape(3, 9 * C1A, C1B), w_small_5b.reshape(3, 9 * C2A, C2B)
-
-    z_in, q, stats, head, tail = call(
+    before, behind = neighbours(x[:224], x[256:480])
+    cot = jnp.stack(gather_from(cot, "clip"))
+
+    z_in, q, stats = call(
         first_project,
-        [((512, IN_OUT), F32), ((512, POOL), F32), ((group, 8, 128), F32),
-         ((256, MID + POOL), BF16), ((256, MID + POOL), BF16)],
-        [], x, w_in_4f, w_pool_4f, scalars=0,
-    )
-    before, after = neighbours(head, tail)
+        [((512, IN_OUT), F32), ((512, POOL), F32), ((group, 8, 128), F32)],
+        [], x, w_in_4f, w_pool_4f, scalars=0, us=4,
+    )
     stats = exchange(stats)
-    z_b, z_p, stats, x2_c, u_mid, u_small, head, tail, moments_a = call(
+    z_b, z_p, stats, x2, m_turned, head, tail, moments_a = call(
         first_hidden,
         [((512, BOUT), F32), ((512, POOL), F32), ((group, 16, 128), F32), ((64, C0), BF16),
-         ((1056, 3 * C1A), BF16), ((1056, 3 * C2A), BF16),
-         ((256, BOUT + POOL), BF16), ((256, BOUT + POOL), BF16), ((2, IN_OUT), F32)],
-        [((1024, MID), F32), ((4, 128, 128), F32)],
-        flags, stats, z_in, q, before, after, mid_4f, small_4f, offsets_4f,
-    )
-    before, after = neighbours(head, tail)
-    x2_c = gather_stream(x2_c)
+         ((MID, 512), BF16),
+         ((224, BOUT + POOL), BF16), ((224, BOUT + POOL), BF16), ((2, IN_OUT), F32)],
+        [((1024, MID), F32), ((1056, 3 * C1A), BF16), ((1056, 3 * C2A), BF16),
+         ((4, 128, 128), F32)],
+        flags, stats, z_in, q, before, behind, w_in_4f, w_pool_4f, mid_4f, small_4f, offsets_4f,
+        us=8,
+    )
+    cot = gather_from(after(cot, z_b), "tm")
     stats = exchange(stats)
-    x2_b, moments_b = call(
+    x2, moments_b = call(
         first_output,
-        [((64, BOUT + POOL), BF16), ((2, BOUT + POOL), F32)],
+        [((64, OUTC), BF16), ((2, BOUT + POOL), F32)],
         [((4, 128, 128), F32)],
-        stats, z_b, z_p, offsets_4f, scalars=0,
-    )
-    x2_b = gather_stream(x2_b)
-    cot = gather_stream(cot)
+        stats, z_b, z_p, x2, offsets_4f, scalars=0, us=3,
+    )
+    x2 = jnp.stack(gather_from(x2, "clip"))
+    head, tail, m_turned = lax.optimization_barrier((head, tail, m_turned, x2))[:3]
+    before, behind = neighbours(head, tail)
+    m_turned = gather_from(m_turned, "tm", back=True)
+    x2 = gather_from(after(x2, *cot), "tm")
     rows, slots = group * 64, (clips * (frames + 1) + 2) * 64
     wide = clips * (frames + 1) * 64
     part = (C1B // frames, C2B // frames, IN_OUT // frames, POOL // frames)
@@ -986,44 +1069,62 @@
          ((slots, 9 * C1A), BF16), ((slots, 9 * C2A), BF16), ((slots, POOL), F32),
          ((slots, BOUT), BF16), ((slots, SECTION_A), BF16), ((part[0] + part[1], wide), BF16),
          ((part[2] + part[3], rows), BF16), ((rows, SECTION_A), F32)],
-        flags, x2_c, x2_b, cot, w_in_5b, w_pool_5b, mid_5b, small_5b, offsets_5b,
+        flags, *x2, *cot, w_in_5b, w_pool_5b, mid_5b, small_5b,
+        offsets_5b, us=35,
     )
     d_b, y_b, d_p, y_p, d_c, stats = call(
         first_errors,
-        [((1024, BOUT), F32), ((1024, BOUT), F32), ((1024, POOL), F32), ((1024, POOL), F32),
-         ((512, C0), F32), ((group, 16, 128), F32)],
-        [], flags, dx2, z_b, z_p, z_in, before, after, moments_a, moments_b, offsets_4f,
+        [((1024, BOUT), BF16), ((1024, BOUT), BF16), ((1024, POOL), BF16), ((1024, POOL), BF16),
+         ((512, C0), BF16), ((group, 16, 128), F32)],
+        [], flags, dx2, z_b, z_p, z_in, before, behind, moments_a, moments_b, offsets_4f,
+        us=5,
     )
     stats = exchange(stats)
-    d_m, stats, sums, g_mid, g_small = call(
+    d_m, stats, sums, errors = call(
         functools.partial(first_hidden_back, cells),
         [((512, MID), F32), ((group, 8, 128), F32), ((16, 128), F32),
-         ((frames, 9, part[0], 3 * C1A), BF16), ((frames, 9, part[1], 3 * C2A), BF16)],
-        [((1056, BOUT), BF16), ((C1B, 512), BF16), ((C2B, 512), BF16)],
-        flags, stats, d_b, y_b, z_in, moments_a, moments_b, offsets_4f, u_mid, u_small,
-        mid_4f, small_4f,
-    )
-    g_mid, g_small = scatter_sum(g_mid), scatter_sum(g_small)
+         ((frames, 448, part[0] + part[1]), BF16)],
+        [((1056, BOUT), BF16)],
+        flags, stats, d_b, y_b, z_in, moments_a, moments_b, offsets_4f, mid_4f, small_4f,
+        us=8,
+    )
+    received = hand_on(errors, "tm")
     stats = exchange(stats)
+    (g_conv,) = call(
+        first_kernel_grad,
+        [((clips, C1A // clips, 27 * part[0] + 27 * part[1] // clips), BF16)],
+        [((frames * 512, 9 * part[0]), BF16), ((frames * 512, 9 * part[1]), BF16),
+         ((MID, frames * 512), BF16)],
+        flags, errors, *received[1:], *m_turned, us=6,
+    )
+    stats = after(stats, g_conv)
+    g_conv = hand_on(g_conv, "clip")
     d_x, g_a, g_off = call(
-        functools.partial(first_input_back, cells),
-        [((512, features.shape[-1]), F32), ((frames, part[2] + part[3], features.shape[-1]), BF16),
-         ((1, 1024), F32)],
+        functools.partial(first_input_back, cells, frames),
+        [((512, features.shape[-1]), F32),
+         ((frames, part[2] + part[3], features.shape[-1]), BF16), ((1, 1024), F32)],
         [((512, SECTION_A), BF16)],
         flags, stats, sums, d_m, d_c, d_p, y_p, z_in, moments_a, moments_b, x, w_in_4f, w_pool_4f,
-    )
-    g_a = scatter_sum(g_a)
-
-    def offsets_first(g, inner, outer):
-        return jnp.transpose(g.reshape(9, outer, 3, inner), (0, 2, 3, 1)).reshape(27, inner, outer)
+        us=6,
+    )
+    g_a = summed(lax.all_to_all(g_a, "tm", 0, 0))
+    g_a = g_a.reshape(clips, (part[2] + part[3]) // clips, -1)
+    g_conv = gather_from(summed(g_conv), "clip")
+    g_a = summed(lax.all_to_all(g_a, "clip", 0, 0))
+    g_a = to_all(g_a, "clip").astype(F32).reshape(part[2] + part[3], -1)
+    g_mid, g_small = call(
+        first_kernel_join,
+        [((27, C1A, part[0]), F32), ((27, C2A, part[1]), F32)],
+        [], flags, *g_conv, us=4,
+    )
 
     return (
         out.reshape(1, 1, 8, 8, OUTC)[:, :, :7, :7],
         d_x.reshape(1, 2, 16, 16, -1)[:, :, :14, :14],
         g_a[: part[2]].T,
         g_a[part[2] :].T,
-        offsets_first(g_mid, C1A, part[0]),
-        offsets_first(g_small, C2A, part[1]),
+        g_mid,
+        g_small,
         g_off[0],
         g_in_5b.T,
         g_pool_5b.T,

time: 303 us -> 234 us (0.77)
  blocking collectives: 44.8 us -> 0 us
  waiting for transfers between devices: 76.3 us -> 57.2 us
  starting transfers between devices: 63.5 us -> 79.9 us
  between operations: 14.3 us -> 1.1 us
  other arithmetic: 13.9 us -> 2.98 us
  Pallas kernels: 71.1 us -> 76.5 us
    psum x1 -> x0, blocking collectives: 30.1 us -> none  [scatter_sum(): return lax.psum(total.astype(BF16), 'clip').astype(F32)]
    psum x1 -> x0, waiting for transfers between devices: 25.6 us -> none  [scatter_sum(): return lax.psum(total.astype(BF16), 'clip').astype(F32)]
    all_to_all x1 -> x0, blocking collectives: 14.7 us -> none  [exchange(): return lax.all_to_all(copies, ('clip', 'tm'), 0, 0)]
    all_to_all x0 -> x3, starting transfers between devices: none -> 12.1 us  [the longest x1 4.61 us: small_group(): g_a = summed(lax.all_to_all(g_a, 'clip', 0, 0))]
    all_to_all x3 -> x4, waiting for transfers between devices: 0.01 us -> 9.72 us  [exchange(): return lax.all_to_all(copies, ('clip', 'tm'), 0, 0)]
    all_to_all x3 -> x4, starting transfers between devices: 15.6 us -> 21.5 us  [exchange(): return lax.all_to_all(copies, ('clip', 'tm'), 0, 0)]
    pallas_call x7 -> x9, Pallas kernels: 71.1 us -> 76.5 us  [call(): pl.pallas_call(body, out_shape=[jax.ShapeDtypeStruct(s, d) for s, d in ou...]
    unnamed x36 -> x68, local copies, waits for them, and re-layouts: 7.94 us -> 11.4 us
  transfers between devices with their start and end apart: 35 -> 35, of which waited for: 14 -> 14; matrix products, arithmetic and copies ran while one was open for 7% -> 4% of each run, Pallas kernels for 17% -> 25%
where the time goes in v2:
time: 234 us; the launch traced here: 233 us
  starting transfers between devices  79.9 us (34%)
  Pallas kernels  76.5 us (33%)
  waiting for transfers between devices  57.2 us (24%)
  local copies, waits for them, and re-layouts  15.5 us (7%)
  other arithmetic  2.98 us (1%)
    pallas_call x9, Pallas kernels, call(): pl.pallas_call(body, out_shape=[jax.ShapeDtypeStruct(s, d) for s, d in ou...  76.5 us
    ppermute x18, waiting for transfers between devices, gather_from(): lax.ppermute(value, axis, [((i + step) % size, i) for i in range(size)])  36.5 us
    ppermute x18, starting transfers between devices, gather_from(): lax.ppermute(value, axis, [((i + step) % size, i) for i in range(size)])  26.9 us
    all_to_all x4, starting transfers between devices, exchange(): return lax.all_to_all(copies, ('clip', 'tm'), 0, 0)  21.5 us
    unnamed x68, local copies, waits for them, and re-layouts  11.4 us
    ppermute x4, starting transfers between devices, neighbours(): return (lax.ppermute(tail, 'tm', up), lax.ppermute(head, 'tm', down))  11.2 us
    all_to_all x4, waiting for transfers between devices, exchange(): return lax.all_to_all(copies, ('clip', 'tm'), 0, 0)  9.72 us
    ppermute x6, waiting for transfers between devices, hand_on(): lax.ppermute(chunks[m], axis, [(i, (i + m) % size) for i in range(size)])  9.52 us
  transfers between devices with their start and end apart: 35, of which 14 were waited for; matrix products, arithmetic and copies ran while one was open for 4% of the time, Pallas kernels for 25%

profile of v2, /device:TPU:0, one launch (start us, length us, event | category | flops | bytes accessed | tf_op | source)
XLA Modules:
  0.0 233.2 jit_solution(17356491941089667839)
XLA Ops:
  1.9 4.9 %collective-permute-start = (bf16[224,528]{1,0:T(8,128)(2,1)S(1)}, bf16[224,528]{1,0:T(8,128)(2,1)S(1)}, u32[]{:S(2)}, u32[]{:S(2)}) collective-permute-start(bf16[224,528]{1,0:T(8,128)(2,1)S(1)} %get-tuple-element.122), channel_id=1, source_target_pairs={{0,1},{1,2},{2,3},{4,5},{5,6},{6,7},{8,9},{9,10},{10,11},{12,13},{... | collective-permute-start | bytes 709640 | tf_op jit(solution)/shard_map/ppermute | solution.py:979
  11.1 8.0 %all-to-all-start = ((f32[16,8,128]{2,1,0:T(8,128)}), f32[16,8,128]{2,1,0:T(8,128)S(1)}, u32[]{:S(2)}, u32[]{:S(2)}) async-start(f32[16,8,128]{2,1,0:T(8,128)} %get-tuple-element.53), calls=%async_computation | async-start | bytes 131072 | tf_op jit(solution)/shard_map/all_to_all | solution.py:972
  19.7 6.9 %all-to-all-done.st_ref = f32[16,8,128]{2,1,0:T(8,128)S(1)} async-done(((f32[16,8,128]{2,1,0:T(8,128)}), f32[16,8,128]{2,1,0:T(8,128)S(1)}, u32[]{:S(2)}, u32[]{:S(2)}) %all-to-all-start) | async-done | bytes 65568 | tf_op jit(solution)/shard_map/all_to_all | solution.py:972
  27.5 8.0 %shard_map.212 = (f32[512,448]{1,0:T(8,128)}, f32[512,128]{1,0:T(8,128)}, f32[16,16,128]{2,1,0:T(8,128)}, bf16[64,256]{1,0:T(8,128)(2,1)}, bf16[192,512]{1,0:T(8...) custom-call(s32[4]{0:T(128)} %pad_add_fusion.flag_ref, ...), custom_call_target="tpu_custom_call" | custom-call | flops 8800000000 | bytes 5316624 | tf_op jit(solution)/shard_map/pallas_call | solution.py:956
  35.5 3.5 %all-to-all-start.1 = ((f32[16,16,128]{2,1,0:T(8,128)}), f32[16,16,128]{2,1,0:T(8,128)S(1)}, u32[]{:S(2)}, u32[]{:S(2)}) async-start(f32[16,16,128]{2,1,0:T(8,128)} %get-tuple-element.56), calls=%async_computation.1 | async-start | bytes 262144 | tf_op jit(solution)/shard_map/all_to_all | solution.py:972
  44.8 3.7 %collective-permute-done.7 = bf16[64,832]{1,0:T(8,128)(2,1)S(1)} collective-permute-done((bf16[64,832]{1,0:T(8,128)(2,1)S(1)}, bf16[64,832]{1,0:T(8,128)(2,1)S(1)}, u32[]{:S(2)}, u32[]{:S(2)}) %collective-permute-start.7) | collective-permute-done | bytes 106528 | tf_op jit(solution)/shard_map/ppermute | solution.py:987
  48.5 3.4 %collective-permute-done.6 = bf16[64,832]{1,0:T(8,128)(2,1)S(1)} collective-permute-done((bf16[64,832]{1,0:T(8,128)(2,1)S(1)}, bf16[64,832]{1,0:T(8,128)(2,1)S(1)}, u32[]{:S(2)}, u32[]{:S(2)}) %collective-permute-start.6) | collective-permute-done | bytes 106528 | tf_op jit(solution)/shard_map/ppermute | solution.py:987
  62.0 4.0 %collective-permute-done.4 = bf16[64,832]{1,0:T(8,128)(2,1)S(1)} collective-permute-done((bf16[64,832]{1,0:T(8,128)(2,1)}, bf16[64,832]{1,0:T(8,128)(2,1)S(1)}, u32[]{:S(2)}, u32[]{:S(2)}) %collective-permute-start.4) | collective-permute-done | bytes 106528 | tf_op jit(solution)/shard_map/ppermute | solution.py:987
  78.6 3.6 %collective-permute-start.14 = (bf16[224,576]{1,0:T(8,128)(2,1)}, bf16[224,576]{1,0:T(8,128)(2,1)S(1)}, u32[]{:S(2)}, u32[]{:S(2)}) collective-permute-start(bf16[224,576]{1,0:T(8,128)(2,1)} %get-tuple-element.68), channel_id=1, source_target_pairs={{0,1},{1,2},{2,3},{4,5},{5,6},{6,7},{8,9},{9,10},{10,11},{12,13},{... | collective-permute-start | bytes 774152 | tf_op jit(solution)/shard_map/ppermute | solution.py:979
  83.7 4.5 %collective-permute-done.11.refs_1_ = bf16[4,64,832]{2,1,0:T(8,128)(2,1)S(1)} collective-permute-done((bf16[4,64,832]{2,1,0:T(8,128)(2,1)S(1)}, bf16[4,64,832]{2,1,0:T(8,128)(2,1)S(1)}, u32[]{:S(2)}, u32[]{:S(2)}) %collective-permute-start.11) | collective-permute-done | bytes 426016 | tf_op jit(solution)/shard_map/ppermute | solution.py:987
  88.2 9.7 %collective-permute-done.12.refs_2_ = bf16[4,64,832]{2,1,0:T(8,128)(2,1)} collective-permute-done((bf16[4,64,832]{2,1,0:T(8,128)(2,1)S(1)}, bf16[4,64,832]{2,1,0:T(8,128)(2,1)}, u32[]{:S(2)}, u32[]{:S(2)}) %collective-permute-start.12) | collective-permute-done | bytes 426016 | tf_op jit(solution)/shard_map/ppermute | solution.py:987
  98.1 34.6 %shard_map.214 = (bf16[64,832]{1,0:T(8,128)(2,1)}, f32[192,832]{1,0:T(8,128)}, f32[112,832]{1,0:T(8,128)}, f32[32,832]{1,0:T(8,128)}, f32[27,160,80]{2,1,0:T(8,1...) custom-call(s32[4]{0:T(128)} %pad_add_fusion.flag_ref, bf16[4,64,832]{2,1,0:T(8,128)(2,1)} %copy-done.5, ...), custom_call_target="tpu_custom_call" | custom-call | flops 38499999744 | bytes 7356432 | tf_op jit(solution)/shard_map/pallas_call | solution.py:956
  133.5 5.2 %shard_map.215 = (bf16[1024,448]{1,0:T(8,128)(2,1)}, bf16[1024,448]{1,0:T(8,128)(2,1)}, bf16[1024,128]{1,0:T(8,128)(2,1)}, bf16[1024,128]{1,0:T(8,128)(2,1)}, bf...) custom-call(s32[4]{0:T(128)} %pad_add_fusion.flag_ref, f32[192,832]{1,0:T(8,128)} %get-tuple-element.64.dx_ref, ...), custom_call_target="tpu_custom_call" | custom-call | flops 5500000256 | bytes 3264528 | tf_op jit(solution)/shard_map/pallas_call | solution.py:956
  138.7 6.5 %all-to-all-start.2 = ((f32[16,16,128]{2,1,0:T(8,128)}), f32[16,16,128]{2,1,0:T(8,128)S(1)}, u32[]{:S(2)}, u32[]{:S(2)}) async-start(f32[16,16,128]{2,1,0:T(8,128)} %get-tuple-element.72), calls=%async_computation.2 | async-start | bytes 262144 | tf_op jit(solution)/shard_map/all_to_all | solution.py:972
  153.8 7.2 %shard_map.216 = (f32[512,192]{1,0:T(8,128)}, f32[16,8,128]{2,1,0:T(8,128)}, f32[16,128]{1,0:T(8,128)}, bf16[4,448,112]{2,1,0:T(8,128)(2,1)}) custom-call(s32[4]{0:T(128)} %pad_add_fusion.flag_ref, f32[16,16,128]{2,1,0:T(8,128)} %copy-done.8, bf16[1024,448]{1,0:T(8,128)(2,1)} %get-tuple-element.73.db_ref, bf16[1024,448]{1,0:T(8,128)(2,1)} %get-tuple-element.74.yb_ref, ...), custom_call_target="tpu_custom_call" | custom-call | flops 8800000000 | bytes 5881872 | tf_op jit(solution)/shard_map/pallas_call | solution.py:956
  166.5 3.5 %all-to-all-start.3 = ((f32[16,8,128]{2,1,0:T(8,128)}), f32[16,8,128]{2,1,0:T(8,128)S(1)}, u32[]{:S(2)}, u32[]{:S(2)}) async-start(f32[16,8,128]{2,1,0:T(8,128)} %get-tuple-element.75), calls=%async_computation.3 | async-start | bytes 131072 | tf_op jit(solution)/shard_map/all_to_all | solution.py:972
  171.5 6.4 %shard_map.217 = bf16[4,40,2376]{2,1,0:T(8,128)(2,1)} custom-call(s32[4]{0:T(128)} %pad_add_fusion.flag_ref, bf16[4,448,112]{2,1,0:T(8,128)(2,1)} %get-tuple-element.76.own_ref, bf16[448,112]{1,0:T(8,128)(2,1)} %copy-done.29, bf16[448,112]{1,0:T(8,128)(2,1)} %copy-done.30, bf16[448,112]{1,0:T(8,128)(2,1)} %copy-done.31, ...), custom_call_target="tpu_custom_call" | custom-call | flops 6600000000 | bytes 1488912 | tf_op jit(solution)/shard_map/pallas_call | solution.py:956
  178.5 5.8 %shard_map.218 = (f32[512,528]{1,0:T(8,128)}, bf16[4,144,528]{2,1,0:T(8,128)(2,1)}, f32[1,1024]{1,0:T(1,128)}) custom-call(s32[4]{0:T(128)} %pad_add_fusion.flag_ref, f32[16,8,128]{2,1,0:T(8,128)} %copy-done.12, f32[16,128]{1,0:T(8,128)} %get-tuple-element.79.sum_ref, f32[512,192]{1,0:T(8,128)} %get-tuple-element.80.dm_ref, ...), custom_call_target="tpu_custom_call" | custom-call | flops 6600000000 | bytes 3328016 | tf_op jit(solution)/shard_map/pallas_call | solution.py:956
  184.3 4.1 %all-to-all-start.4 = ((bf16[4,144,528]{2,1,0:T(8,128)(2,1)}), bf16[4,144,528]{2,1,0:T(8,128)(2,1)S(1)}, u32[]{:S(2)}, u32[]{:S(2)}) async-start(bf16[4,144,528]{2,1,0:T(8,128)(2,1)} %get-tuple-element.85), calls=%async_computation.4 | async-start | bytes 1474560 | tf_op jit(solution)/shard_map/all_to_all | solution.py:1110
  197.0 4.6 %all-to-all-start.5 = ((bf16[4,36,528]{2,1,0:T(8,128)(2,1)}), bf16[4,36,528]{2,1,0:T(8,128)(2,1)S(1)}, u32[]{:S(2)}, u32[]{:S(2)}) async-start(bf16[4,36,528]{2,1,0:T(8,128)(2,1)} %add.45), calls=%async_computation.5 | async-start | bytes 409600 | tf_op jit(solution)/shard_map/all_to_all | solution.py:1113
  201.6 9.5 %collective-permute-done.23 = bf16[40,2376]{1,0:T(8,128)(2,1)} collective-permute-done((bf16[40,2376]{1,0:T(8,128)(2,1)S(1)}, bf16[40,2376]{1,0:T(8,128)(2,1)}, u32[]{:S(2)}, u32[]{:S(2)}) %collective-permute-start.23) | collective-permute-done | bytes 190112 | tf_op jit(solution)/shard_map/ppermute | solution.py:995
  212.4 4.4 %collective-permute-start.26 = (bf16[40,2376]{1,0:T(8,128)(2,1)S(1)}, bf16[40,2376]{1,0:T(8,128)(2,1)S(1)}, u32[]{:S(2)}, u32[]{:S(2)}) collective-permute-start(bf16[40,2376]{1,0:T(8,128)(2,1)S(1)} %fusion.2.refs_0_), channel_id=1, source_target_pairs={{8,0},{12,4},{0,8},{4,12},{9,1},{13,5},{1,9},{5,13},{10,2},{14,6},... | collective-permute-start | bytes 570248 | tf_op jit(solution)/shard_map/ppermute | solution.py:987
  222.9 3.7 %collective-permute-done.26.refs_2_ = bf16[40,2376]{1,0:T(8,128)(2,1)S(1)} collective-permute-done((bf16[40,2376]{1,0:T(8,128)(2,1)S(1)}, bf16[40,2376]{1,0:T(8,128)(2,1)S(1)}, u32[]{:S(2)}, u32[]{:S(2)}) %collective-permute-start.26) | collective-permute-done | bytes 190112 | tf_op jit(solution)/shard_map/ppermute | solution.py:987
  228.0 3.7 %shard_map.219 = (f32[27,160,80]{2,1,0:T(8,128)}, f32[27,32,32]{2,1,0:T(8,128)}) custom-call(s32[4]{0:T(128)} %pad_add_fusion.flag_ref, bf16[40,2376]{1,0:T(8,128)(2,1)} %copy-done.6, bf16[40,2376]{1,0:T(8,128)(2,1)} %copy-done.26, bf16[40,2376]{1,0:T(8,128)(2,1)} %copy-done.27, bf16[40,2376]{1,0:T(8,128)(2,1)} %copy-done.28), custom_call_target="tpu_custom_call" | custom-call | flops 4400000000 | bytes 760336 | tf_op jit(solution)/shard_map/pallas_call | solution.py:956
  (141 shorter events, 72.5 us)
Async XLA Ops:
  1.9 24.8 %collective-permute-start = (bf16[224,528]{1,0:T(8,128)(2,1)S(1)}, bf16[224,528]{1,0:T(8,128)(2,1)S(1)}, u32[]{:S(2)}, u32[]{:S(2)}) collective-permute-start(bf16[224,528]{1,0:T(8,128)(2,1)S(1)} %get-tuple-element.122), channel_id=1, source_target_pairs={{0,1},{1,2},{2,3},{4,5},{5,6},{6,7},{8,9},{9,10},{10,11},{12,13},{... | collective-permute-start | bytes 709640 | tf_op jit(solution)/shard_map/ppermute | solution.py:979
  6.8 19.9 %collective-permute-start.1 = (bf16[224,528]{1,0:T(8,128)(2,1)S(1)}, bf16[224,528]{1,0:T(8,128)(2,1)S(1)}, u32[]{:S(2)}, u32[]{:S(2)}) collective-permute-start(bf16[224,528]{1,0:T(8,128)(2,1)S(1)} %get-tuple-element.121), channel_id=1, source_target_pairs={{1,0},{2,1},{3,2},{5,4},{6,5},{7,6},{9,8},{10,9},{11,10},{13,12},{... | collective-permute-start | bytes 709640 | tf_op jit(solution)/shard_map/ppermute | solution.py:979
  11.1 15.6 %all-to-all-start = ((f32[16,8,128]{2,1,0:T(8,128)}), f32[16,8,128]{2,1,0:T(8,128)S(1)}, u32[]{:S(2)}, u32[]{:S(2)}) async-start(f32[16,8,128]{2,1,0:T(8,128)} %get-tuple-element.53), calls=%async_computation | async-start | bytes 131072 | tf_op jit(solution)/shard_map/all_to_all | solution.py:972
  35.5 20.1 %all-to-all-start.1 = ((f32[16,16,128]{2,1,0:T(8,128)}), f32[16,16,128]{2,1,0:T(8,128)S(1)}, u32[]{:S(2)}, u32[]{:S(2)}) async-start(f32[16,16,128]{2,1,0:T(8,128)} %get-tuple-element.56), calls=%async_computation.1 | async-start | bytes 262144 | tf_op jit(solution)/shard_map/all_to_all | solution.py:972
  52.0 20.0 %collective-permute-start.8 = (bf16[4,64,832]{2,1,0:T(8,128)(2,1)S(1)}, bf16[4,64,832]{2,1,0:T(8,128)(2,1)S(1)}, u32[]{:S(2)}, u32[]{:S(2)}) collective-permute-start(bf16[4,64,832]{2,1,0:T(8,128)(2,1)S(1)} %pad_maximum_fusion.1.refs_4_), channel_id=1, source_target_pairs={{1,0},{2,1},{3,2},{0,3},{5,4},{6,5},{7,6},{4,7},{9,8},{10,9},{11,1... | collective-permute-start | bytes 1277960 | tf_op jit(solution)/shard_map/ppermute | solution.py:987
  54.5 20.3 %collective-permute-start.9 = (bf16[4,64,832]{2,1,0:T(8,128)(2,1)S(1)}, bf16[4,64,832]{2,1,0:T(8,128)(2,1)S(1)}, u32[]{:S(2)}, u32[]{:S(2)}) collective-permute-start(bf16[4,64,832]{2,1,0:T(8,128)(2,1)S(1)} %pad_maximum_fusion.1.refs_4_), channel_id=1, source_target_pairs={{2,0},{3,1},{0,2},{1,3},{6,4},{7,5},{4,6},{5,7},{10,8},{11,9},{8,1... | collective-permute-start | bytes 1277960 | tf_op jit(solution)/shard_map/ppermute | solution.py:987
  55.0 19.7 %collective-permute-start.10 = (bf16[4,64,832]{2,1,0:T(8,128)(2,1)S(1)}, bf16[4,64,832]{2,1,0:T(8,128)(2,1)S(1)}, u32[]{:S(2)}, u32[]{:S(2)}) collective-permute-start(bf16[4,64,832]{2,1,0:T(8,128)(2,1)S(1)} %pad_maximum_fusion.1.refs_4_), channel_id=1, source_target_pairs={{3,0},{0,1},{1,2},{2,3},{7,4},{4,5},{5,6},{6,7},{11,8},{8,9},{9,10... | collective-permute-start | bytes 1277960 | tf_op jit(solution)/shard_map/ppermute | solution.py:987
  74.7 13.5 %collective-permute-start.11 = (bf16[4,64,832]{2,1,0:T(8,128)(2,1)S(1)}, bf16[4,64,832]{2,1,0:T(8,128)(2,1)S(1)}, u32[]{:S(2)}, u32[]{:S(2)}) collective-permute-start(bf16[4,64,832]{2,1,0:T(8,128)(2,1)S(1)} %pad_maximum_fusion.refs_0_), channel_id=1, source_target_pairs={{1,0},{2,1},{3,2},{0,3},{5,4},{6,5},{7,6},{4,7},{9,8},{10,9},{11,1... | collective-permute-start | bytes 1277960 | tf_op jit(solution)/shard_map/ppermute | solution.py:987
  75.3 22.6 %collective-permute-start.12 = (bf16[4,64,832]{2,1,0:T(8,128)(2,1)S(1)}, bf16[4,64,832]{2,1,0:T(8,128)(2,1)}, u32[]{:S(2)}, u32[]{:S(2)}) collective-permute-start(bf16[4,64,832]{2,1,0:T(8,128)(2,1)S(1)} %pad_maximum_fusion.refs_0_), channel_id=1, source_target_pairs={{2,0},{3,1},{0,2},{1,3},{6,4},{7,5},{4,6},{5,7},{10,8},{11,9},{8,1... | collective-permute-start | bytes 1277960 | tf_op jit(solution)/shard_map/ppermute | solution.py:987
  76.5 21.5 %collective-permute-start.13 = (bf16[4,64,832]{2,1,0:T(8,128)(2,1)S(1)}, bf16[4,64,832]{2,1,0:T(8,128)(2,1)}, u32[]{:S(2)}, u32[]{:S(2)}) collective-permute-start(bf16[4,64,832]{2,1,0:T(8,128)(2,1)S(1)} %pad_maximum_fusion.refs_0_), channel_id=1, source_target_pairs={{3,0},{0,1},{1,2},{2,3},{7,4},{4,5},{5,6},{6,7},{11,8},{8,9},{9,10... | collective-permute-start | bytes 1277960 | tf_op jit(solution)/shard_map/ppermute | solution.py:987
  78.6 54.1 %collective-permute-start.14 = (bf16[224,576]{1,0:T(8,128)(2,1)}, bf16[224,576]{1,0:T(8,128)(2,1)S(1)}, u32[]{:S(2)}, u32[]{:S(2)}) collective-permute-start(bf16[224,576]{1,0:T(8,128)(2,1)} %get-tuple-element.68), channel_id=1, source_target_pairs={{0,1},{1,2},{2,3},{4,5},{5,6},{6,7},{8,9},{9,10},{10,11},{12,13},{... | collective-permute-start | bytes 774152 | tf_op jit(solution)/shard_map/ppermute | solution.py:979
  82.2 50.5 %collective-permute-start.15 = (bf16[224,576]{1,0:T(8,128)(2,1)S(1)}, bf16[224,576]{1,0:T(8,128)(2,1)S(1)}, u32[]{:S(2)}, u32[]{:S(2)}) collective-permute-start(bf16[224,576]{1,0:T(8,128)(2,1)S(1)} %copy-done.17), channel_id=1, source_target_pairs={{1,0},{2,1},{3,2},{5,4},{6,5},{7,6},{9,8},{10,9},{11,10},{13,12},{... | collective-permute-start | bytes 774152 | tf_op jit(solution)/shard_map/ppermute | solution.py:979
  138.7 14.4 %all-to-all-start.2 = ((f32[16,16,128]{2,1,0:T(8,128)}), f32[16,16,128]{2,1,0:T(8,128)S(1)}, u32[]{:S(2)}, u32[]{:S(2)}) async-start(f32[16,16,128]{2,1,0:T(8,128)} %get-tuple-element.72), calls=%async_computation.2 | async-start | bytes 262144 | tf_op jit(solution)/shard_map/all_to_all | solution.py:972
  145.3 18.3 %collective-permute-start.19 = (bf16[192,512]{1,0:T(8,128)(2,1)S(1)}, bf16[192,512]{1,0:T(8,128)(2,1)S(1)}, u32[]{:S(2)}, u32[]{:S(2)}) collective-permute-start(bf16[192,512]{1,0:T(8,128)(2,1)S(1)} %copy-done.22), channel_id=1, source_target_pairs={{3,0},{0,1},{1,2},{2,3},{7,4},{4,5},{5,6},{6,7},{11,8},{8,9},{9,10... | collective-permute-start | bytes 589832 | tf_op jit(solution)/shard_map/ppermute | solution.py:987
  147.5 22.5 %collective-permute-start.20 = (bf16[192,512]{1,0:T(8,128)(2,1)S(1)}, bf16[192,512]{1,0:T(8,128)(2,1)S(1)}, u32[]{:S(2)}, u32[]{:S(2)}) collective-permute-start(bf16[192,512]{1,0:T(8,128)(2,1)S(1)} %copy-done.22), channel_id=1, source_target_pairs={{2,0},{3,1},{0,2},{1,3},{6,4},{7,5},{4,6},{5,7},{10,8},{11,9},{8,1... | collective-permute-start | bytes 589832 | tf_op jit(solution)/shard_map/ppermute | solution.py:987
  148.9 21.1 %collective-permute-start.21 = (bf16[192,512]{1,0:T(8,128)(2,1)S(1)}, bf16[192,512]{1,0:T(8,128)(2,1)S(1)}, u32[]{:S(2)}, u32[]{:S(2)}) collective-permute-start(bf16[192,512]{1,0:T(8,128)(2,1)S(1)} %copy-done.22), channel_id=1, source_target_pairs={{1,0},{2,1},{3,2},{0,3},{5,4},{6,5},{7,6},{4,7},{9,8},{10,9},{11,1... | collective-permute-start | bytes 589832 | tf_op jit(solution)/shard_map/ppermute | solution.py:987
  166.5 11.4 %all-to-all-start.3 = ((f32[16,8,128]{2,1,0:T(8,128)}), f32[16,8,128]{2,1,0:T(8,128)S(1)}, u32[]{:S(2)}, u32[]{:S(2)}) async-start(f32[16,8,128]{2,1,0:T(8,128)} %get-tuple-element.75), calls=%async_computation.3 | async-start | bytes 131072 | tf_op jit(solution)/shard_map/all_to_all | solution.py:972
  184.3 11.9 %all-to-all-start.4 = ((bf16[4,144,528]{2,1,0:T(8,128)(2,1)}), bf16[4,144,528]{2,1,0:T(8,128)(2,1)S(1)}, u32[]{:S(2)}, u32[]{:S(2)}) async-start(bf16[4,144,528]{2,1,0:T(8,128)(2,1)} %get-tuple-element.85), calls=%async_computation.4 | async-start | bytes 1474560 | tf_op jit(solution)/shard_map/all_to_all | solution.py:1110
  188.5 13.1 %collective-permute-start.24 = (bf16[40,2376]{1,0:T(8,128)(2,1)S(1)}, bf16[40,2376]{1,0:T(8,128)(2,1)}, u32[]{:S(2)}, u32[]{:S(2)}) collective-permute-start(bf16[40,2376]{1,0:T(8,128)(2,1)S(1)} %get-tuple-element.119), channel_id=1, source_target_pairs={{0,12},{4,0},{8,4},{12,8},{1,13},{5,1},{9,5},{13,9},{2,14},{6,2},{... | collective-permute-start | bytes 570248 | tf_op jit(solution)/shard_map/ppermute | solution.py:995
  191.8 19.3 %collective-permute-start.23 = (bf16[40,2376]{1,0:T(8,128)(2,1)S(1)}, bf16[40,2376]{1,0:T(8,128)(2,1)}, u32[]{:S(2)}, u32[]{:S(2)}) collective-permute-start(bf16[40,2376]{1,0:T(8,128)(2,1)S(1)} %get-tuple-element.120), channel_id=1, source_target_pairs={{0,8},{4,12},{8,0},{12,4},{1,9},{5,13},{9,1},{13,5},{2,10},{6,14},... | collective-permute-start | bytes 570248 | tf_op jit(solution)/shard_map/ppermute | solution.py:995
  191.8 19.3 %collective-permute-start.22 = (bf16[40,2376]{1,0:T(8,128)(2,1)S(1)}, bf16[40,2376]{1,0:T(8,128)(2,1)}, u32[]{:S(2)}, u32[]{:S(2)}) collective-permute-start(bf16[40,2376]{1,0:T(8,128)(2,1)S(1)} %get-tuple-element.118), channel_id=1, source_target_pairs={{0,4},{4,8},{8,12},{12,0},{1,5},{5,9},{9,13},{13,1},{2,6},{6,10},{... | collective-permute-start | bytes 570248 | tf_op jit(solution)/shard_map/ppermute | solution.py:995
  197.0 21.8 %all-to-all-start.5 = ((bf16[4,36,528]{2,1,0:T(8,128)(2,1)}), bf16[4,36,528]{2,1,0:T(8,128)(2,1)S(1)}, u32[]{:S(2)}, u32[]{:S(2)}) async-start(bf16[4,36,528]{2,1,0:T(8,128)(2,1)} %add.45), calls=%async_computation.5 | async-start | bytes 409600 | tf_op jit(solution)/shard_map/all_to_all | solution.py:1113
  212.4 14.2 %collective-permute-start.26 = (bf16[40,2376]{1,0:T(8,128)(2,1)S(1)}, bf16[40,2376]{1,0:T(8,128)(2,1)S(1)}, u32[]{:S(2)}, u32[]{:S(2)}) collective-permute-start(bf16[40,2376]{1,0:T(8,128)(2,1)S(1)} %fusion.2.refs_0_), channel_id=1, source_target_pairs={{8,0},{12,4},{0,8},{4,12},{9,1},{13,5},{1,9},{5,13},{10,2},{14,6},... | collective-permute-start | bytes 570248 | tf_op jit(solution)/shard_map/ppermute | solution.py:987
  219.5 12.2 %all-to-all-start.6 = ((bf16[4,36,528]{2,1,0:T(8,128)(2,1)}), bf16[4,36,528]{2,1,0:T(8,128)(2,1)S(1)}, u32[]{:S(2)}, u32[]{:S(2)}) async-start(bf16[4,36,528]{2,1,0:T(8,128)(2,1)} %broadcast_in_dim.17), calls=%async_computation.6 | async-start | bytes 409600 | tf_op jit(solution)/shard_map/all_to_all | solution.py:1001
  (43 other events, 346.3 us)
